TPU v7x, 256 devices: a whole 4x4x8 slice. The times are simulated.
256 devices in a mesh: sec: 32 (over x, y, core), mpo: 8 (over z).
Axes of the slice: x: 4, y: 4, z: 8, core: 2. Of those that a mesh axis runs over, the one named last changes fastest.
Arguments:
- wavefunction: float32 [128, 256, 256], P('sec')
- left_env: float32 [40, 128, 256, 256], P('mpo', 'sec')
- right_env: float32 [40, 128, 256, 256], P('mpo', 'sec')
- sector_dims: int32 [128, 2], P('sec'), may hold values from 64 to 256, as said below
- charges: int32 [128, 2], replicated, may hold values from 0 to 15, as said below
- term_class: int32 [40], P('mpo'), may hold values from 0 to 4
Outputs:
- residual: float32 [128, 256, 256], P('sec', 'mpo')
- applied: float32 [128, 256, 256], P('sec', 'mpo')
Inputs may be any that keep to these rules, and one draw needn't show every extreme that they name: `charges`: column 0 is a particle-number label n and column 1 a spin label s; every pair with n below 16 and s below 8 is held by exactly one slot; slots k * 4 to (k + 1) * 4 - 1 belong to device k along sec, and 8 n + s minus that device index is the same modulo the number of devices along sec for all slots. `sector_dims`: column 0 is a sector's dimension on the left of the two-site matrix, column 1 on the right; entries of a block outside them are not part of the state.
All inputs are finite; a program needn't handle non-finite values.
Results may differ from a plain program's by a relative error of at most 0.0017.
Values sent between devices are 32-bit elements; how exact they have to be, the bound alone decides.
No kernel may reach another device: no remote copies, remote signals or barrier semaphores. Data moves between devices by JAX's collectives and lax.ppermute only.
A program may use at most 64 MiB of HBM per device.

v0:
```python
import jax
import jax.numpy as jnp
from jax import lax
from jax.sharding import PartitionSpec as P

number_steps = (0, 1, 1, -1, -1)
spin_steps = (0, 1, -1, 1, -1)
precise = lax.Precision.HIGHEST


def passed_along(value, axis, by):
    count = lax.axis_size(axis)
    return lax.ppermute(value, axis, [(i, (i + by) % count) for i in range(count)])


def block_mask(sector_dims, block_size):
    positions = jnp.arange(block_size)
    row_live = positions[None, :, None] < sector_dims[:, 0][:, None, None]
    col_live = positions[None, None, :] < sector_dims[:, 1][:, None, None]
    return (row_live & col_live).astype(jnp.float32)


def pick_sources(received, own_charges, sender_charges, charge_kind):
    matches = (
        sender_charges[None, :, 0] == own_charges[:, None, 0] - number_steps[charge_kind]
    ) & (sender_charges[None, :, 1] == own_charges[:, None, 1] - spin_steps[charge_kind])
    return jnp.einsum("ik,krc->irc", matches.astype(jnp.float32), received, precision=precise)


def gather_sources(blocks, charges, transfer, sec_dev):
    devices_sec = lax.axis_size("sec")
    device_here = lax.axis_index("sec")
    own_charges = lax.dynamic_slice_in_dim(charges, device_here * sec_dev, sec_dev, 0)
    picked = [blocks]
    for charge_kind in range(1, 5):
        distance = (8 * number_steps[charge_kind] + spin_steps[charge_kind]) % devices_sec
        received = transfer(blocks, distance)
        sender = (device_here - distance) % devices_sec
        sender_charges = lax.dynamic_slice_in_dim(charges, sender * sec_dev, sec_dev, 0)
        picked.append(pick_sources(received, own_charges, sender_charges, charge_kind))
    return jnp.stack(picked)


def apply_terms(stacked, left_env, right_env, term_class):

    def add_term(term, totals):
        source = lax.dynamic_index_in_dim(stacked, term_class[term], 0, keepdims=False)
        left_block = lax.dynamic_index_in_dim(left_env, term, 0, keepdims=False)
        right_block = lax.dynamic_index_in_dim(right_env, term, 0, keepdims=False)
        middle = jnp.einsum("irk,ikc->irc", left_block, source, precision=precise)
        return totals + jnp.einsum("irk,ick->irc", middle, right_block, precision=precise)

    return lax.fori_loop(0, left_env.shape[0], add_term, jnp.zeros(stacked.shape[1:], jnp.float32))


def local(wavefunction, left_env, right_env, sector_dims, charges, term_class):
    sec_dev = wavefunction.shape[0]
    block_size = wavefunction.shape[1]
    share_rows = block_size // lax.axis_size("mpo")
    first_row = lax.axis_index("mpo") * share_rows
    live_mask = block_mask(sector_dims, block_size)
    masked = live_mask * wavefunction
    mask_rows = lax.dynamic_slice_in_dim(live_mask, first_row, share_rows, 1)
    masked_rows = lax.dynamic_slice_in_dim(masked, first_row, share_rows, 1)

    def shift_first(blocks, distance):
        return passed_along(blocks, "sec", distance)

    def shift_second(blocks, distance):
        return passed_along(blocks, "sec", distance)

    stacked = gather_sources(masked, charges, shift_first, sec_dev)
    first_part = apply_terms(stacked, left_env, right_env, term_class)
    sigma_full = lax.psum(first_part, "mpo") * live_mask
    correlation, weight = lax.psum((jnp.sum(masked * sigma_full), jnp.sum(masked * masked)), "sec")
    quotient = correlation / weight
    sigma_rows = lax.dynamic_slice_in_dim(sigma_full, first_row, share_rows, 1)
    operand = sigma_full - quotient * masked
    second = gather_sources(operand, charges, shift_second, sec_dev)
    residual_rows = sigma_rows - quotient * masked_rows
    second_part = apply_terms(second, left_env, right_env, term_class)
    applied_rows = lax.psum_scatter(second_part, "mpo", scatter_dimension=1, tiled=True) * mask_rows
    return (residual_rows, applied_rows)


def solution(mesh):
    placed = (
        P("sec", None, None),
        P("mpo", "sec", None, None),
        P("mpo", "sec", None, None),
        P("sec", None),
        P(),
        P("mpo"),
    )
    return jax.shard_map(
        local,
        mesh=mesh,
        in_specs=placed,
        out_specs=(P("sec", "mpo", None), P("sec", "mpo", None)),
        check_vma=False,
    )
```

profile of v0, /device:TPU:2, one launch (start us, length us, event | category | flops | bytes accessed | tf_op | source)
XLA Modules:
  0.0 457.2 jit_solution(4583705038414648888)
XLA Ops:
  7.2 0.8 slice_bitcast_fusion.9
  8.1 3.2 bitcast_dynamic-update-slice_fusion.1
  11.3 0.9 collective-permute-start
  12.2 3.6 collective-permute-start.1
  15.8 3.8 collective-permute-start.3
  19.6 0.9 constant_dynamic-slice_fusion.2
  20.7 17.6 %collective-permute-done = f32[4,256,256]{2,0,1:T(4,128)} collective-permute-done((f32[4,256,256]{2,0,1:T(4,128)S(1)}, f32[4,256,256]{2,0,1:T(4,128)}, u32[]{:S(2)}, u32[]{:S(2)}) %collective-permute-start) | collective-permute-done | bytes 1048608 | tf_op jit(solution)/shard_map/ppermute | solution.py:13
  38.3 3.3 fusion.21
  41.6 18.6 %collective-permute-done.1 = f32[4,256,256]{2,0,1:T(4,128)} collective-permute-done((f32[4,256,256]{2,0,1:T(4,128)S(1)}, f32[4,256,256]{2,0,1:T(4,128)}, u32[]{:S(2)}, u32[]{:S(2)}) %collective-permute-start.1) | collective-permute-done | bytes 1048608 | tf_op jit(solution)/shard_map/ppermute | solution.py:13
  60.1 3.3 fusion.20
  63.4 3.3 fusion.19
  66.7 2.0 fusion.18
  68.7 45.4 %while.28 = (s32[]{:T(128)}, f32[4,256,256]{2,1,0:T(8,128)S(1)}, f32[5,4,256,256]{3,2,1,0:T(8,128)}, s32[5]{0:T(128)S(1)}, f32[5,4,256,256]{3,1,2,0:T(4,128)}, /...) while((s32[]{:T(128)}, f32[4,256,256]{2,1,0:T(8,128)S(1)}, ...), condition=%wide.region_1.2_spmd.clone, body=%wide.region_0.1_spmd.clone.sunk | while | flops 1611137024 | bytes 9437353 | solution.py:53
  71.3 1.4 constant_dynamic-slice_fusion.9
  72.7 2.5 fusion.51
  75.2 2.6 convolution_add_fusion.4
  80.3 1.4 constant_dynamic-slice_fusion.9
  81.8 2.5 fusion.51
  84.2 2.6 convolution_add_fusion.4
  89.4 1.4 constant_dynamic-slice_fusion.9
  90.9 2.5 fusion.51
  93.3 2.6 convolution_add_fusion.4
  98.5 1.4 constant_dynamic-slice_fusion.9
  99.9 2.5 fusion.51
  102.4 2.6 convolution_add_fusion.4
  107.6 1.4 constant_dynamic-slice_fusion.9
  109.0 2.5 fusion.51
  111.5 2.6 convolution_add_fusion.4
  114.2 1.7 copy.17
  115.9 84.9 %all-reduce.5.cloned.1.call-done = f32[4,256,256]{2,0,1:T(4,128)} async-done(((f32[4,256,256]{2,0,1:T(4,128)}), f32[4,256,256]{2,0,1:T(4,128)}) %all-reduce.5.cloned.1.call-update) | async-done | bytes 1048592 | tf_op jit(solution)/shard_map/psum | solution.py:74
  200.8 2.6 multiply_reduce_fusion
  203.4 53.6 %all-reduce.1 = (f32[]{:T(128)}, f32[]{:T(128)}) all-reduce(f32[]{:T(128)} %get-tuple-element.293, f32[]{:T(128)} %get-tuple-element.292), channel_id=1, replica_groups=mesh['sec'=32,'mpo'=8] {'sec'}, use_global_device_ids=true, to_apply=%region_4.5 | all-reduce | flops 2 | bytes 16 | tf_op jit(solution)/shard_map/psum | solution.py:75
  258.4 1.3 bitcast_dynamic-update-slice_fusion
  259.7 0.9 collective-permute-start.4
  260.7 3.5 collective-permute-start.5
  264.2 5.6 %collective-permute-start.6 = (f32[4,256,256]{2,0,1:T(4,128)S(1)}, f32[4,256,256]{2,0,1:T(4,128)}, u32[]{:S(2)}, u32[]{:S(2)}) collective-permute-start(f32[4,256,256]{2,0,1:T(4,128)S(1)} %get-tuple-element.321), channel_id=1, source_target_pairs={{0,200},{8,208},{16,216},{24,224},{32,232},{40,240},{48,248},{56,0... | collective-permute-start | bytes 3145736 | tf_op jit(solution)/shard_map/ppermute | solution.py:13
  269.8 4.5 collective-permute-start.7
  274.2 11.5 %collective-permute-done.4 = f32[4,256,256]{2,0,1:T(4,128)} collective-permute-done((f32[4,256,256]{2,0,1:T(4,128)S(1)}, f32[4,256,256]{2,0,1:T(4,128)}, u32[]{:S(2)}, u32[]{:S(2)}) %collective-permute-start.4) | collective-permute-done | bytes 1048608 | tf_op jit(solution)/shard_map/ppermute | solution.py:13
  285.7 3.3 fusion.17
  289.0 26.2 %collective-permute-done.5 = f32[4,256,256]{2,0,1:T(4,128)} collective-permute-done((f32[4,256,256]{2,0,1:T(4,128)S(1)}, f32[4,256,256]{2,0,1:T(4,128)}, u32[]{:S(2)}, u32[]{:S(2)}) %collective-permute-start.5) | collective-permute-done | bytes 1048608 | tf_op jit(solution)/shard_map/ppermute | solution.py:13
  315.3 3.3 fusion.16
  318.5 3.3 fusion.15
  321.8 3.3 fusion.14
  325.1 45.4 %while.29 = (s32[]{:T(128)}, f32[4,256,256]{2,1,0:T(8,128)S(1)}, f32[5,4,256,256]{3,2,1,0:T(8,128)}, s32[5]{0:T(128)S(1)}, f32[5,4,256,256]{3,1,2,0:T(4,128)}, /...) while((s32[]{:T(128)}, f32[4,256,256]{2,1,0:T(8,128)S(1)}, ...), condition=%wide.region_8.9_spmd.clone, body=%wide.region_7.8_spmd.clone.sunk | while | flops 1611137024 | bytes 9437353 | solution.py:53
  327.6 1.4 constant_dynamic-slice_fusion.10
  329.0 2.5 fusion.55
  331.5 2.6 convolution_add_fusion.5
  336.7 1.4 constant_dynamic-slice_fusion.10
  338.1 2.5 fusion.55
  340.6 2.6 convolution_add_fusion.5
  345.8 1.4 constant_dynamic-slice_fusion.10
  347.2 2.5 fusion.55
  349.7 2.6 convolution_add_fusion.5
  354.9 1.4 constant_dynamic-slice_fusion.10
  356.3 2.5 fusion.55
  358.8 2.6 convolution_add_fusion.5
  363.9 1.4 constant_dynamic-slice_fusion.10
  365.4 2.5 fusion.55
  367.8 2.6 convolution_add_fusion.5
  370.5 1.7 copy.19
  373.9 0.9 multiply_subtract_fusion.1
  374.9 0.7 copy.20
  375.5 73.1 %all-reduce.7.cloned.1.call-done = f32[4,256,256]{2,0,1:T(4,128)} async-done(((f32[4,256,256]{2,0,1:T(4,128)}), f32[4,256,256]{2,0,1:T(4,128)}) %all-reduce.7.cloned.1.call-update) | async-done | bytes 1048592
  448.7 0.9 dynamic-slice_multiply_fusion
  (36 shorter events, 7.9 us)
Async XLA Ops:
  7.2 193.6 %all-reduce.5.cloned.1.call-start = ((), (), s32[]{:S(2)}) async-start(), calls=%async_computation | async-start | bytes 2097152 | tf_op jit(solution)/shard_map/psum | solution.py:74
  8.1 60.7 %copy-start.1 = (s32[5]{0:T(128)S(1)}, s32[5]{0:T(128)}, u32[]{:S(2)}) copy-start(s32[5]{0:T(128)} %param.15) | copy-start | bytes 64
  11.3 27.0 %collective-permute-start = (f32[4,256,256]{2,0,1:T(4,128)S(1)}, f32[4,256,256]{2,0,1:T(4,128)}, u32[]{:S(2)}, u32[]{:S(2)}) collective-permute-start(f32[4,256,256]{2,0,1:T(4,128)S(1)} %get-tuple-element.324), channel_id=1, source_target_pairs={{0,72},{8,80},{16,88},{24,96},{32,104},{40,112},{48,120},{56,128},... | collective-permute-start | bytes 3145736 | tf_op jit(solution)/shard_map/ppermute | solution.py:13
  12.2 47.9 %collective-permute-start.1 = (f32[4,256,256]{2,0,1:T(4,128)S(1)}, f32[4,256,256]{2,0,1:T(4,128)}, u32[]{:S(2)}, u32[]{:S(2)}) collective-permute-start(f32[4,256,256]{2,0,1:T(4,128)S(1)} %get-tuple-element.324), channel_id=1, source_target_pairs={{0,56},{8,64},{16,72},{24,80},{32,88},{40,96},{48,104},{56,112},{6... | collective-permute-start | bytes 3145736 | tf_op jit(solution)/shard_map/ppermute | solution.py:13
  15.8 47.6 %collective-permute-start.2 = (f32[4,256,256]{2,0,1:T(4,128)S(1)}, f32[4,256,256]{2,0,1:T(4,128)}, u32[]{:S(2)}, u32[]{:S(2)}) collective-permute-start(f32[4,256,256]{2,0,1:T(4,128)S(1)} %get-tuple-element.324), channel_id=1, source_target_pairs={{0,200},{8,208},{16,216},{24,224},{32,232},{40,240},{48,248},{56,0... | collective-permute-start | bytes 3145736 | tf_op jit(solution)/shard_map/ppermute | solution.py:13
  15.8 50.9 %collective-permute-start.3 = (f32[4,256,256]{2,0,1:T(4,128)S(1)}, f32[4,256,256]{2,0,1:T(4,128)S(1)}, u32[]{:S(2)}, u32[]{:S(2)}) collective-permute-start(f32[4,256,256]{2,0,1:T(4,128)S(1)} %get-tuple-element.324), channel_id=1, source_target_pairs={{0,184},{8,192},{16,200},{24,208},{32,216},{40,224},{48,232},{56,2... | collective-permute-start | bytes 3145736 | tf_op jit(solution)/shard_map/ppermute | solution.py:13
  115.9 332.8 %all-reduce.7.cloned.1.call-start = ((), (), s32[]{:S(2)}) async-start(), calls=%async_computation.1 | async-start | bytes 2097152
  203.4 70.8 %copy-start = (f32[4,256,256]{2,0,1:T(4,128)}, f32[4,256,256]{2,0,1:T(4,128)S(1)}, u32[]{:S(2)}) copy-start(f32[4,256,256]{2,0,1:T(4,128)S(1)} %get-tuple-element.322) | copy-start | bytes 3145732
  259.7 26.0 %collective-permute-start.4 = (f32[4,256,256]{2,0,1:T(4,128)S(1)}, f32[4,256,256]{2,0,1:T(4,128)}, u32[]{:S(2)}, u32[]{:S(2)}) collective-permute-start(f32[4,256,256]{2,0,1:T(4,128)S(1)} %get-tuple-element.321), channel_id=1, source_target_pairs={{0,72},{8,80},{16,88},{24,96},{32,104},{40,112},{48,120},{56,128},... | collective-permute-start | bytes 3145736 | tf_op jit(solution)/shard_map/ppermute | solution.py:13
  260.7 54.6 %collective-permute-start.5 = (f32[4,256,256]{2,0,1:T(4,128)S(1)}, f32[4,256,256]{2,0,1:T(4,128)}, u32[]{:S(2)}, u32[]{:S(2)}) collective-permute-start(f32[4,256,256]{2,0,1:T(4,128)S(1)} %get-tuple-element.321), channel_id=1, source_target_pairs={{0,56},{8,64},{16,72},{24,80},{32,88},{40,96},{48,104},{56,112},{6... | collective-permute-start | bytes 3145736 | tf_op jit(solution)/shard_map/ppermute | solution.py:13
  264.2 54.3 %collective-permute-start.6 = (f32[4,256,256]{2,0,1:T(4,128)S(1)}, f32[4,256,256]{2,0,1:T(4,128)}, u32[]{:S(2)}, u32[]{:S(2)}) collective-permute-start(f32[4,256,256]{2,0,1:T(4,128)S(1)} %get-tuple-element.321), channel_id=1, source_target_pairs={{0,200},{8,208},{16,216},{24,224},{32,232},{40,240},{48,248},{56,0... | collective-permute-start | bytes 3145736 | tf_op jit(solution)/shard_map/ppermute | solution.py:13
  269.8 52.0 %collective-permute-start.7 = (f32[4,256,256]{2,0,1:T(4,128)S(1)}, f32[4,256,256]{2,0,1:T(4,128)}, u32[]{:S(2)}, u32[]{:S(2)}) collective-permute-start(f32[4,256,256]{2,0,1:T(4,128)S(1)} %get-tuple-element.321), channel_id=1, source_target_pairs={{0,184},{8,192},{16,200},{24,208},{32,216},{40,224},{48,232},{56,2... | collective-permute-start | bytes 3145736 | tf_op jit(solution)/shard_map/ppermute | solution.py:13
  325.1 47.2 %copy-start.2 = (u32[256]{0:T(256)S(1)}, u32[256]{0:T(256)}, u32[]{:S(2)}) copy-start(u32[256]{0:T(256)} %constant.143) | copy-start | bytes 3076
Sparse Core Ops, SparseCore 0:
  116.0 84.7 all-reduce.4
  372.3 76.3 all-reduce.6
where the time goes:
time: 459 us; the launch traced here: 457 us
  waiting for transfers between devices  232 us (51%)
  matrix products  76.1 us (17%)
  blocking collectives  53.6 us (12%)
  local copies, waits for them, and re-layouts  27 us (6%)
  starting transfers between devices  22.9 us (5%)
  loops' own time  19.8 us (4%)
  between operations  16.1 us (4%)
  other arithmetic  9.71 us (2%)
    psum x1, waiting for transfers between devices, local(): sigma_full = lax.psum(first_part, 'mpo') * live_mask  84.9 us
    ppermute x8, waiting for transfers between devices, passed_along(): lax.ppermute(value, axis, [(i, (i + by) % count) for i in range(count)])  74 us
    unnamed x3, waiting for transfers between devices  73.2 us
    psum x1, blocking collectives, local(): lax.psum((jnp.sum(masked * sigma_full), jnp.sum(masked * masked)), 'sec')  53.6 us
    dot_general x10, matrix products, add_term(): jnp.einsum('irk,ick->irc', middle, right_block, precision=precise)  26.4 us
    dot_general x8, matrix products, pick_sources(): jnp.einsum('ik,krc->irc', matches.astype(jnp.float32), received, precisio...  24.9 us
    dot_general x10, matrix products, add_term(): middle = jnp.einsum('irk,ikc->irc', left_block, source, precision=precise)  24.8 us
    ppermute x8, starting transfers between devices, passed_along(): lax.ppermute(value, axis, [(i, (i + by) % count) for i in range(count)])  22.8 us
  transfers between devices with their start and end apart: 10, of which 6 were waited for; matrix products, arithmetic and copies ran while one was open for 5% of the time, Pallas kernels for 0%

commit v1 on v0

v1 whole, which is shorter than its diff:
```python
import functools
import jax
import jax.numpy as jnp
from jax import lax
from jax.experimental import pallas as pl
from jax.experimental.pallas import tpu as pltpu
from jax.sharding import PartitionSpec as P

number_steps = (0, 1, 1, -1, -1)
spin_steps = (0, 1, -1, 1, -1)
SPINS = 8
RANK, SLOT, SOURCE, LIVE, ROWS, COLS, TERM, PLANE, META = 0, 8, 16, 40, 64, 72, 80, 96, 128


def passed_along(value, axis, by):
    count = lax.axis_size(axis)
    return lax.ppermute(value, axis, [(i, (i + by) % count) for i in range(count)])


def plan_kernel(numbers, charges_ref, dims_ref, term_ref, meta_ref):
    sec_dev = dims_ref.shape[0]
    first = lax.axis_index("sec") * sec_dev
    spin = charges_ref[first, 1]
    residue = charges_ref[first, 0] % (numbers // sec_dev)
    stride = numbers // sec_dev
    for slot in range(sec_dev):
        rank = charges_ref[first + slot, 0] // stride
        meta_ref[RANK + slot] = rank
        meta_ref[SLOT + rank] = slot
        meta_ref[ROWS + rank] = dims_ref[slot, 0]
        meta_ref[COLS + rank] = dims_ref[slot, 1]
    for rank in range(sec_dev):
        number = residue + stride * rank
        for kind in range(5):
            source_number = number - number_steps[kind]
            source_spin = spin - spin_steps[kind]
            inside = (source_number >= 0) & (source_number < numbers) & (source_spin >= 0) & (source_spin < SPINS)
            meta_ref[SOURCE + kind * sec_dev + rank] = jnp.where(inside, source_number // stride, rank)
            meta_ref[LIVE + kind * sec_dev + rank] = jnp.where(inside, 1, 0)
    for term in range(term_ref.shape[0]):
        meta_ref[TERM + term] = term_ref[term]
    meta_ref[PLANE] = lax.axis_index("mpo")


def make_plan(charges, sector_dims, term_class):
    sec_dev = sector_dims.shape[0]
    numbers = charges.shape[0] // SPINS
    return pl.pallas_call(
        functools.partial(plan_kernel, numbers),
        out_shape=jax.ShapeDtypeStruct((META,), jnp.int32),
        in_specs=[pl.BlockSpec(memory_space=pltpu.SMEM)] * 3,
        out_specs=pl.BlockSpec(memory_space=pltpu.SMEM),
    )(charges, sector_dims, term_class)


def live_area(shape, first_row, rows, cols):
    row = lax.broadcasted_iota(jnp.int32, shape, len(shape) - 2) + first_row
    col = lax.broadcasted_iota(jnp.int32, shape, len(shape) - 1)
    return (row < rows) & (col < cols)


def mask_kernel(meta_ref, block_ref, out_ref):
    rank = meta_ref[RANK + pl.program_id(0)]
    block = block_ref[0]
    live = live_area(block.shape, 0, meta_ref[ROWS + rank], meta_ref[COLS + rank])
    out_ref[...] = jnp.where(live, block, 0.0).reshape(out_ref.shape)


def mask_and_sort(meta, wavefunction, planes):
    sec_dev, size, _ = wavefunction.shape
    share = size // planes
    return pl.pallas_call(
        mask_kernel,
        out_shape=jax.ShapeDtypeStruct((planes, sec_dev, share, size), jnp.float32),
        grid_spec=pltpu.PrefetchScalarGridSpec(
            num_scalar_prefetch=1,
            grid=(sec_dev,),
            in_specs=[pl.BlockSpec((1, size, size), lambda i, meta: (i, 0, 0))],
            out_specs=pl.BlockSpec((planes, 1, share, size), lambda i, meta: (0, meta[RANK + i], 0, 0)),
        ),
    )(meta, wavefunction)


def split(value):
    high = value.astype(jnp.bfloat16)
    return high, (value - high.astype(jnp.float32)).astype(jnp.bfloat16)


def product(a, b, contract):
    dims = (((1,), (contract,)), ((), ()))
    dot = functools.partial(lax.dot_general, dimension_numbers=dims, preferred_element_type=jnp.float32)
    return dot(a[0], b[0]) + (dot(a[0], b[1]) + dot(a[1], b[0]))


def terms_kernel(sec_dev, meta_ref, *refs):
    sources, (left_ref, right_ref, out_ref, high_ref, low_ref) = refs[:5], refs[5:]
    rank = pl.program_id(0)
    size = left_ref.shape[-1]
    for kind in range(5):
        live = meta_ref[LIVE + kind * sec_dev + rank] != 0
        high, low = split(jnp.where(live, sources[kind][...].reshape(size, size), 0.0))
        high_ref[kind] = high
        low_ref[kind] = low
    total = None
    for term in range(left_ref.shape[0]):
        kind = meta_ref[TERM + term]
        middle = product(split(left_ref[term, 0]), (high_ref[kind], low_ref[kind]), 0)
        part = product(split(middle), split(right_ref[term, 0]), 1)
        total = part if total is None else total + part
    out_ref[...] = total.reshape(out_ref.shape)


def apply_terms(meta, sources, left_env, right_env):
    planes, sec_dev, share, size = sources[0].shape
    terms = left_env.shape[0]

    def source_spec(kind):
        return pl.BlockSpec(
            (planes, 1, share, size), lambda j, meta: (0, meta[SOURCE + kind * sec_dev + j], 0, 0)
        )

    env_spec = pl.BlockSpec((terms, 1, size, size), lambda j, meta: (0, meta[SLOT + j], 0, 0))
    return pl.pallas_call(
        functools.partial(terms_kernel, sec_dev),
        out_shape=jax.ShapeDtypeStruct((planes, sec_dev, share, size), jnp.float32),
        grid_spec=pltpu.PrefetchScalarGridSpec(
            num_scalar_prefetch=1,
            grid=(sec_dev,),
            in_specs=[source_spec(kind) for kind in range(5)] + [env_spec, env_spec],
            out_specs=pl.BlockSpec((planes, 1, share, size), lambda j, meta: (0, j, 0, 0)),
            scratch_shapes=[pltpu.VMEM((5, size, size), jnp.bfloat16)] * 2,
        ),
        compiler_params=pltpu.CompilerParams(vmem_limit_bytes=40 * 2**20),
        cost_estimate=pl.CostEstimate(
            flops=sec_dev * terms * 12 * size**3, bytes_accessed=4 * sec_dev * size * size * (2 * terms + 6), transcendentals=0
        ),
    )(meta, *sources, left_env, right_env)


def sum_kernel(meta_ref, parts_ref, masked_ref, sigma_ref, sums_ref):
    rank = pl.program_id(0)
    share = sigma_ref.shape[1]
    total = jnp.sum(parts_ref[:, 0], axis=0)
    live = live_area(total.shape, meta_ref[PLANE] * share, meta_ref[ROWS + rank], meta_ref[COLS + rank])
    sigma = jnp.where(live, total, 0.0)
    sigma_ref[0] = sigma
    masked = masked_ref[0, 0]

    @pl.when(rank == 0)
    def _():
        sums_ref[...] = jnp.zeros_like(sums_ref)

    def folded(value):
        return jnp.sum(value.reshape(share // 8, 8, value.shape[1]), axis=0)

    sums_ref[0] += folded(masked * sigma)
    sums_ref[1] += folded(masked * masked)


def sum_parts(meta, parts, masked):
    planes, sec_dev, share, size = parts.shape
    return pl.pallas_call(
        sum_kernel,
        out_shape=(
            jax.ShapeDtypeStruct((sec_dev, share, size), jnp.float32),
            jax.ShapeDtypeStruct((2, 8, size), jnp.float32),
        ),
        grid_spec=pltpu.PrefetchScalarGridSpec(
            num_scalar_prefetch=1,
            grid=(sec_dev,),
            in_specs=[
                pl.BlockSpec((planes, 1, share, size), lambda j, meta: (0, j, 0, 0)),
                pl.BlockSpec((1, 1, share, size), lambda j, meta: (meta[PLANE], j, 0, 0)),
            ],
            out_specs=(
                pl.BlockSpec((1, share, size), lambda j, meta: (j, 0, 0)),
                pl.BlockSpec((2, 8, size), lambda j, meta: (0, 0, 0)),
            ),
        ),
    )(meta, parts, masked)


def final_kernel(meta_ref, parts_ref, sigma_ref, masked_ref, sums_ref, residual_ref, applied_ref):
    rank = pl.program_id(0)
    share = sigma_ref.shape[1]
    quotient = jnp.sum(sums_ref[0], keepdims=True) / jnp.sum(sums_ref[1], keepdims=True)
    total = jnp.sum(parts_ref[:, 0], axis=0)
    live = live_area(total.shape, meta_ref[PLANE] * share, meta_ref[ROWS + rank], meta_ref[COLS + rank])
    sigma = sigma_ref[0]
    residual_ref[0] = sigma - quotient * masked_ref[0, 0]
    applied_ref[0] = jnp.where(live, total, 0.0) - quotient * sigma


def finish(meta, parts, sigma, masked, sums):
    planes, sec_dev, share, size = parts.shape
    out_spec = pl.BlockSpec((1, share, size), lambda j, meta: (meta[SLOT + j], 0, 0))
    return pl.pallas_call(
        final_kernel,
        out_shape=(jax.ShapeDtypeStruct((sec_dev, share, size), jnp.float32),) * 2,
        grid_spec=pltpu.PrefetchScalarGridSpec(
            num_scalar_prefetch=1,
            grid=(sec_dev,),
            in_specs=[
                pl.BlockSpec((planes, 1, share, size), lambda j, meta: (0, j, 0, 0)),
                pl.BlockSpec((1, share, size), lambda j, meta: (j, 0, 0)),
                pl.BlockSpec((1, 1, share, size), lambda j, meta: (meta[PLANE], j, 0, 0)),
                pl.BlockSpec((2, 8, size), lambda j, meta: (0, 0, 0)),
            ],
            out_specs=(out_spec, out_spec),
        ),
    )(meta, parts, sigma, masked, sums)


def from_neighbours(blocks):
    steps = [(SPINS * dn + ds) for dn, ds in zip(number_steps, spin_steps)]
    return [blocks] + [passed_along(blocks, "sec", step) for step in steps[1:]]


def summed_over_devices(value):
    for axis in ("mpo", "sec"):
        count = lax.axis_size(axis)
        step = 1
        while step < count:
            value = value + passed_along(value, axis, step)
            step *= 2
    return value


def local(wavefunction, left_env, right_env, sector_dims, charges, term_class):
    planes = lax.axis_size("mpo")
    meta = make_plan(charges, sector_dims, term_class)
    masked = mask_and_sort(meta, wavefunction, planes)
    first = apply_terms(meta, from_neighbours(masked), left_env, right_env)
    sigma, sums = sum_parts(meta, lax.all_to_all(first, "mpo", 0, 0), masked)
    sigma_full = lax.all_gather(sigma, "mpo", axis=0)
    sums = summed_over_devices(sums)
    second = apply_terms(meta, from_neighbours(sigma_full), left_env, right_env)
    return finish(meta, lax.all_to_all(second, "mpo", 0, 0), sigma, masked, sums)


def solution(mesh):
    placed = (
        P("sec", None, None),
        P("mpo", "sec", None, None),
        P("mpo", "sec", None, None),
        P("sec", None),
        P(),
        P("mpo"),
    )
    return jax.shard_map(
        local,
        mesh=mesh,
        in_specs=placed,
        out_specs=(P("sec", "mpo", None), P("sec", "mpo", None)),
        check_vma=False,
    )
```

time: 459 us -> 310 us (0.68)
  matrix products: 76.1 us -> 0 us
  waiting for transfers between devices: 232 us -> 175 us
  Pallas kernels: 0 us -> 34.4 us
  loops' own time: 19.8 us -> 0 us
  blocking collectives: 53.6 us -> 37.8 us
  local copies, waits for them, and re-layouts: 27 us -> 11.8 us
  starting transfers between devices: 22.9 us -> 33.5 us
  other arithmetic: 9.71 us -> 0.64 us
    psum x1 -> x0, waiting for transfers between devices: 84.9 us -> none  [local(): sigma_full = lax.psum(first_part, 'mpo') * live_mask]
    dot_general x28 -> x0, matrix products: 76.1 us -> none  [the longest x10 26.4 us: add_term(): jnp.einsum('irk,ick->irc', middle, right_block, precision=precise)]
    unnamed x3 -> x1, waiting for transfers between devices: 73.2 us -> 0.02 us
    ppermute x8 -> x16, waiting for transfers between devices: 74 us -> 141 us  [passed_along(): lax.ppermute(value, axis, [(i, (i + by) % count) for i in range(count)])]
    psum x1 -> x0, blocking collectives: 53.6 us -> none  [local(): lax.psum((jnp.sum(masked * sigma_full), jnp.sum(masked * masked)), 'sec')]
    all_to_all x0 -> x1, blocking collectives: none -> 37.8 us  [local(): sigma, sums = sum_parts(meta, lax.all_to_all(first, 'mpo', 0, 0), masked)]
    pallas_call x0 -> x6, Pallas kernels: none -> 34.4 us  [the longest x2 19.8 us: apply_terms(): pl.pallas_call(functools.partial(terms_kernel, sec_dev), out_shape=jax.Sh...]
    all_gather x0 -> x1, waiting for transfers between devices: none -> 33.6 us  [local(): sigma_full = lax.all_gather(sigma, 'mpo', axis=0)]
  transfers between devices with their start and end apart: 10 -> 18, of which waited for: 6 -> 15; matrix products, arithmetic and copies ran while one was open for 5% -> 0% of each run, Pallas kernels for 0% -> 0%
where the time goes in v1:
time: 310 us; the launch traced here: 307 us
  waiting for transfers between devices  175 us (56%)
  blocking collectives  37.8 us (12%)
  Pallas kernels  34.4 us (11%)
  starting transfers between devices  33.5 us (11%)
  between operations  14.1 us (5%)
  local copies, waits for them, and re-layouts  11.8 us (4%)
    ppermute x16, waiting for transfers between devices, passed_along(): lax.ppermute(value, axis, [(i, (i + by) % count) for i in range(count)])  141 us
    all_to_all x1, blocking collectives, local(): sigma, sums = sum_parts(meta, lax.all_to_all(first, 'mpo', 0, 0), masked)  37.8 us
    all_gather x1, waiting for transfers between devices, local(): sigma_full = lax.all_gather(sigma, 'mpo', axis=0)  33.6 us
    ppermute x16, starting transfers between devices, passed_along(): lax.ppermute(value, axis, [(i, (i + by) % count) for i in range(count)])  29.3 us
    pallas_call x2, Pallas kernels, apply_terms(): pl.pallas_call(functools.partial(terms_kernel, sec_dev), out_shape=jax.Sh...  19.8 us
    unnamed x18, local copies, waits for them, and re-layouts  11.8 us
  transfers between devices with their start and end apart: 18, of which 15 were waited for; matrix products, arithmetic and copies ran while one was open for 0% of the time, Pallas kernels for 0%

profile of v1, /device:TPU:2, one launch (start us, length us, event | category | flops | bytes accessed | tf_op | source)
XLA Modules:
  0.0 306.9 jit_solution(13360454845372791139)
XLA Ops:
  7.2 0.0 all-gather.3.cloned.1.call-start
  7.2 1.3 copy.11.dims_ref
  8.5 1.4 copy.10.charges_ref
  10.0 2.4 shard_map.77.meta_ref
  12.4 0.0 copy-start.5
  12.4 4.1 %shard_map.78.refs_0_.masked_ref = f32[8,4,32,256]{3,2,1,0:T(8,128)} custom-call(s32[128]{0:T(128)} %shard_map.77.meta_ref, f32[4,256,256]{2,1,0:T(8,128)} %block_ref.1), custom_call_target="tpu_custom_call" | custom-call | tf_op jit(solution)/shard_map/pallas_call | solution.py:72
  16.5 4.0 %collective-permute-start.3 = (f32[8,4,32,256]{3,2,1,0:T(8,128)}, f32[8,4,32,256]{3,2,1,0:T(8,128)S(1)}, u32[]{:S(2)}, u32[]{:S(2)}) collective-permute-start(f32[8,4,32,256]{3,2,1,0:T(8,128)} %shard_map.78.refs_0_.masked_ref), channel_id=1, source_target_pairs={{0,184},{8,192},{16,200},{24,208},{32,216},{40,224},{48,232},{56,2... | collective-permute-start | bytes 3145736 | tf_op jit(solution)/shard_map/ppermute | solution.py:17
  20.5 0.0 collective-permute-start.2
  20.5 3.0 collective-permute-start.1
  23.5 0.0 collective-permute-start
  23.5 27.3 %collective-permute-done.3.refs_4_ = f32[8,4,32,256]{3,2,1,0:T(8,128)S(1)} collective-permute-done((f32[8,4,32,256]{3,2,1,0:T(8,128)}, f32[8,4,32,256]{3,2,1,0:T(8,128)S(1)}, u32[]{:S(2)}, u32[]{:S(2)}) %collective-permute-start.3) | collective-permute-done | bytes 1048608 | tf_op jit(solution)/shard_map/ppermute | solution.py:17
  50.8 14.1 %collective-permute-done.2.refs_3_ = f32[8,4,32,256]{3,2,1,0:T(8,128)S(1)} collective-permute-done((f32[8,4,32,256]{3,2,1,0:T(8,128)}, f32[8,4,32,256]{3,2,1,0:T(8,128)S(1)}, u32[]{:S(2)}, u32[]{:S(2)}) %collective-permute-start.2) | collective-permute-done | bytes 1048608 | tf_op jit(solution)/shard_map/ppermute | solution.py:17
  64.9 0.0 collective-permute-done.1.refs_2_
  64.9 2.9 collective-permute-done.refs_1_
  67.8 0.0 copy-start
  67.8 2.5 copy-done
  70.3 0.0 copy-start.2
  70.3 1.2 copy-done.2
  71.5 0.0 copy-start.4
  71.5 0.7 copy-done.4
  72.2 9.6 %shard_map.79 = f32[8,4,32,256]{3,2,1,0:T(8,128)S(1)} custom-call(s32[128]{0:T(128)S(1)} %copy-done.4, f32[8,4,32,256]{3,2,1,0:T(8,128)S(1)} %copy-done.2, f32[8,4,32,256]{3,2,1,0:T(8,128)S(1)} %collective-permute-done.refs_1_, f32[8,4,32,256]{3,2,1,0:T(8,128)S(1)} %collective-permute-done.1.refs_2_, f32[8,4,32,256]{3,2,1,0:T(8,128)S(1)} %collective-permute-done.2.refs_3_, ...), custom_call_target="tpu_custom_call" | custom-call | flops 4026531840 | bytes 16777216 | tf_op jit(solution)/shard_map/pallas_call | solution.py:123
  81.8 37.8 %all_to_all.10.parts_ref = f32[8,4,32,256]{3,2,1,0:T(8,128)} all-to-all(f32[8,4,32,256]{3,2,1,0:T(8,128)S(1)} %shard_map.79), channel_id=1, replica_groups=mesh['sec'=32,'mpo'=8] {'mpo'}, dimensions={0} | all-to-all | bytes 2097152 | tf_op jit(solution)/shard_map/all_to_all | solution.py:234
  119.7 3.9 %shard_map.80 = (f32[4,32,256]{2,1,0:T(8,128)}, f32[2,8,256]{2,1,0:T(8,128)}) custom-call(s32[128]{0:T(128)} %shard_map.77.meta_ref, f32[8,4,32,256]{3,2,1,0:T(8,128)} %all_to_all.10.parts_ref, f32[8,4,32,256]{3,2,1,0:T(8,128)} %shard_map.78.refs_0_.masked_ref), custom_call_target="tpu_custom_call" | custom-call | tf_op jit(solution)/shard_map/pallas_call | solution.py:162
  123.5 0.0 copy-start.7
  123.5 0.0 all-gather.3.cloned.1.call-update
  123.6 33.6 %all-gather.3.cloned.1.call-done = f32[32,32,256]{2,1,0:T(8,128)} async-done(((f32[4,32,256]{2,1,0:T(8,128)}), f32[32,32,256]{2,1,0:T(8,128)}) %all-gather.3.cloned.1.call-update) | async-done | bytes 1048592 | tf_op jit(solution)/shard_map/all_gather | solution.py:235
  157.1 0.0 collective-permute-start.7
  157.1 3.0 collective-permute-start.6
  160.1 0.1 collective-permute-start.5
  160.2 0.5 collective-permute-start.4
  160.6 32.7 %collective-permute-done.7.refs_4_ = f32[8,4,32,256]{3,2,1,0:T(8,128)S(1)} collective-permute-done((f32[8,4,32,256]{3,2,1,0:T(8,128)}, f32[8,4,32,256]{3,2,1,0:T(8,128)S(1)}, u32[]{:S(2)}, u32[]{:S(2)}) %collective-permute-start.7) | collective-permute-done | bytes 1048608 | tf_op jit(solution)/shard_map/ppermute | solution.py:17
  193.3 11.2 %collective-permute-done.6.refs_3_ = f32[8,4,32,256]{3,2,1,0:T(8,128)S(1)} collective-permute-done((f32[8,4,32,256]{3,2,1,0:T(8,128)}, f32[8,4,32,256]{3,2,1,0:T(8,128)S(1)}, u32[]{:S(2)}, u32[]{:S(2)}) %collective-permute-start.6) | collective-permute-done | bytes 1048608 | tf_op jit(solution)/shard_map/ppermute | solution.py:17
  204.5 0.0 collective-permute-done.5.refs_2_
  204.5 3.5 %collective-permute-done.4.refs_1_ = f32[8,4,32,256]{3,2,1,0:T(8,128)S(1)} collective-permute-done((f32[8,4,32,256]{3,2,1,0:T(8,128)}, f32[8,4,32,256]{3,2,1,0:T(8,128)S(1)}, u32[]{:S(2)}, u32[]{:S(2)}) %collective-permute-start.4) | collective-permute-done | bytes 1048608 | tf_op jit(solution)/shard_map/ppermute | solution.py:17
  208.1 0.0 copy-done.5
  208.1 0.0 copy-start.1
  208.1 2.5 copy-done.1
  210.6 0.0 copy-start.3
  210.6 1.2 copy-done.3
  211.8 10.2 %shard_map.81 = f32[8,4,32,256]{3,2,1,0:T(8,128)} custom-call(s32[128]{0:T(128)S(1)} %copy-done.5, f32[8,4,32,256]{3,2,1,0:T(8,128)S(1)} %bitcast.5, f32[8,4,32,256]{3,2,1,0:T(8,128)S(1)} %collective-permute-done.4.refs_1_, f32[8,4,32,256]{3,2,1,0:T(8,128)S(1)} %collective-permute-done.5.refs_2_, f32[8,4,32,256]{3,2,1,0:T(8,128)S(1)} %collective-permute-done.6.refs_3_, ...), custom_call_target="tpu_custom_call" | custom-call | flops 4026531840 | bytes 16777216 | tf_op jit(solution)/shard_map/pallas_call | solution.py:123
  222.0 4.2 %all-to-all-start.1 = ((f32[8,4,32,256]{3,2,1,0:T(8,128)}), f32[8,4,32,256]{3,2,1,0:T(8,128)S(1)}, u32[]{:S(2)}, u32[]{:S(2)}) async-start(f32[8,4,32,256]{3,2,1,0:T(8,128)} %shard_map.81), calls=%async_computation.1 | async-start | bytes 2097152 | tf_op jit(solution)/shard_map/all_to_all | solution.py:238
  226.2 0.0 copy-done.7
  226.2 2.0 collective-permute-start.8
  228.3 19.9 %collective-permute-done.8 = f32[2,8,256]{2,1,0:T(8,128)S(1)} collective-permute-done((f32[2,8,256]{2,1,0:T(8,128)S(1)}, f32[2,8,256]{2,1,0:T(8,128)S(1)}, u32[]{:S(2)}, u32[]{:S(2)}) %collective-permute-start.8) | collective-permute-done | bytes 16416 | tf_op jit(solution)/shard_map/ppermute | solution.py:17
  248.1 4.6 %collective-permute-start.9 = (f32[2,8,256]{2,1,0:T(8,128)S(1)}, f32[2,8,256]{2,1,0:T(8,128)S(1)}, u32[]{:S(2)}, u32[]{:S(2)}) collective-permute-start(f32[2,8,256]{2,1,0:T(8,128)S(1)} %add.24), channel_id=1, source_target_pairs={{0,2},{1,3},{2,4},{3,5},{4,6},{5,7},{6,0},{7,1},{8,10},{9,11},{10,... | collective-permute-start | bytes 49160 | tf_op jit(solution)/shard_map/ppermute | solution.py:17
  252.7 2.7 collective-permute-done.9
  255.4 7.5 %collective-permute-start.10 = (f32[2,8,256]{2,1,0:T(8,128)S(1)}, f32[2,8,256]{2,1,0:T(8,128)S(1)}, u32[]{:S(2)}, u32[]{:S(2)}) collective-permute-start(f32[2,8,256]{2,1,0:T(8,128)S(1)} %add.25), channel_id=1, source_target_pairs={{0,4},{1,5},{2,6},{3,7},{4,0},{5,1},{6,2},{7,3},{8,12},{9,13},{10,... | collective-permute-start | bytes 49160 | tf_op jit(solution)/shard_map/ppermute | solution.py:17
  262.9 1.7 collective-permute-done.10
  264.6 0.0 collective-permute-start.11
  264.6 5.3 %collective-permute-done.11 = f32[2,8,256]{2,1,0:T(8,128)S(1)} collective-permute-done((f32[2,8,256]{2,1,0:T(8,128)S(1)}, f32[2,8,256]{2,1,0:T(8,128)S(1)}, u32[]{:S(2)}, u32[]{:S(2)}) %collective-permute-start.11) | collective-permute-done | bytes 16416 | tf_op jit(solution)/shard_map/ppermute | solution.py:17
  269.9 0.0 collective-permute-start.12
  269.9 6.0 %collective-permute-done.12 = f32[2,8,256]{2,1,0:T(8,128)S(1)} collective-permute-done((f32[2,8,256]{2,1,0:T(8,128)S(1)}, f32[2,8,256]{2,1,0:T(8,128)S(1)}, u32[]{:S(2)}, u32[]{:S(2)}) %collective-permute-start.12) | collective-permute-done | bytes 16416 | tf_op jit(solution)/shard_map/ppermute | solution.py:17
  275.9 0.0 collective-permute-start.13
  275.9 6.1 %collective-permute-done.13 = f32[2,8,256]{2,1,0:T(8,128)S(1)} collective-permute-done((f32[2,8,256]{2,1,0:T(8,128)S(1)}, f32[2,8,256]{2,1,0:T(8,128)S(1)}, u32[]{:S(2)}, u32[]{:S(2)}) %collective-permute-start.13) | collective-permute-done | bytes 16416 | tf_op jit(solution)/shard_map/ppermute | solution.py:17
  282.1 2.9 collective-permute-start.14
  285.0 4.1 %collective-permute-done.14 = f32[2,8,256]{2,1,0:T(8,128)S(1)} collective-permute-done((f32[2,8,256]{2,1,0:T(8,128)S(1)}, f32[2,8,256]{2,1,0:T(8,128)S(1)}, u32[]{:S(2)}, u32[]{:S(2)}) %collective-permute-start.14) | collective-permute-done | bytes 16416 | tf_op jit(solution)/shard_map/ppermute | solution.py:17
  289.1 1.8 collective-permute-start.15
  290.9 3.4 %collective-permute-done.15 = f32[2,8,256]{2,1,0:T(8,128)S(1)} collective-permute-done((f32[2,8,256]{2,1,0:T(8,128)S(1)}, f32[2,8,256]{2,1,0:T(8,128)S(1)}, u32[]{:S(2)}, u32[]{:S(2)}) %collective-permute-start.15) | collective-permute-done | bytes 16416 | tf_op jit(solution)/shard_map/ppermute | solution.py:17
  294.3 0.6 add.31.sums_ref
  294.9 0.0 all-to-all-done.1.parts_ref
  294.9 0.0 copy-start.6
  294.9 1.0 copy-done.6
  295.9 4.1 %shard_map.82 = (f32[4,32,256]{2,1,0:T(8,128)}, f32[4,32,256]{2,1,0:T(8,128)}) custom-call(s32[128]{0:T(128)} %shard_map.77.meta_ref, f32[8,4,32,256]{3,2,1,0:T(8,128)} %copy-done.6, f32[4,32,256]{2,1,0:T(8,128)} %get-tuple-element.4.sigma_ref, f32[8,4,32,256]{3,2,1,0:T(8,128)} %shard_map.78.refs_0_.masked_ref, f32[2,8,256]{2,1,0:T(8,128)} %add.31.sums_ref), custom_call_target="tpu_custom_call" | custom-call | tf_op jit(solution)/shard_map/pallas_call | solution.py:197
  (7 shorter events, 0.0 us)
Async XLA Ops:
  7.2 150.0 %all-gather.3.cloned.1.call-start = ((), (), s32[]{:S(2)}) async-start(), calls=%async_computation.2 | async-start | bytes 1179648 | tf_op jit(solution)/shard_map/all_gather | solution.py:235
  12.4 195.7 %copy-start.5 = (s32[128]{0:T(128)S(1)}, s32[128]{0:T(128)}, u32[]{:S(2)}) copy-start(s32[128]{0:T(128)} %shard_map.77.meta_ref) | copy-start | bytes 1540
  16.5 34.3 %collective-permute-start.3 = (f32[8,4,32,256]{3,2,1,0:T(8,128)}, f32[8,4,32,256]{3,2,1,0:T(8,128)S(1)}, u32[]{:S(2)}, u32[]{:S(2)}) collective-permute-start(f32[8,4,32,256]{3,2,1,0:T(8,128)} %shard_map.78.refs_0_.masked_ref), channel_id=1, source_target_pairs={{0,184},{8,192},{16,200},{24,208},{32,216},{40,224},{48,232},{56,2... | collective-permute-start | bytes 3145736 | tf_op jit(solution)/shard_map/ppermute | solution.py:17
  20.5 44.4 %collective-permute-start.2 = (f32[8,4,32,256]{3,2,1,0:T(8,128)}, f32[8,4,32,256]{3,2,1,0:T(8,128)S(1)}, u32[]{:S(2)}, u32[]{:S(2)}) collective-permute-start(f32[8,4,32,256]{3,2,1,0:T(8,128)} %shard_map.78.refs_0_.masked_ref), channel_id=1, source_target_pairs={{0,200},{8,208},{16,216},{24,224},{32,232},{40,240},{48,248},{56,0... | collective-permute-start | bytes 3145736 | tf_op jit(solution)/shard_map/ppermute | solution.py:17
  20.5 44.4 %collective-permute-start.1 = (f32[8,4,32,256]{3,2,1,0:T(8,128)}, f32[8,4,32,256]{3,2,1,0:T(8,128)S(1)}, u32[]{:S(2)}, u32[]{:S(2)}) collective-permute-start(f32[8,4,32,256]{3,2,1,0:T(8,128)} %shard_map.78.refs_0_.masked_ref), channel_id=1, source_target_pairs={{0,56},{8,64},{16,72},{24,80},{32,88},{40,96},{48,104},{56,112},{6... | collective-permute-start | bytes 3145736 | tf_op jit(solution)/shard_map/ppermute | solution.py:17
  23.5 44.4 %collective-permute-start = (f32[8,4,32,256]{3,2,1,0:T(8,128)}, f32[8,4,32,256]{3,2,1,0:T(8,128)S(1)}, u32[]{:S(2)}, u32[]{:S(2)}) collective-permute-start(f32[8,4,32,256]{3,2,1,0:T(8,128)} %shard_map.78.refs_0_.masked_ref), channel_id=1, source_target_pairs={{0,72},{8,80},{16,88},{24,96},{32,104},{40,112},{48,120},{56,128},... | collective-permute-start | bytes 3145736 | tf_op jit(solution)/shard_map/ppermute | solution.py:17
  67.8 2.5 copy-start
  70.3 1.2 copy-start.2
  71.5 0.7 copy-start.4
  123.5 102.7 %copy-start.7 = (f32[2,8,256]{2,1,0:T(8,128)S(1)}, f32[2,8,256]{2,1,0:T(8,128)}, u32[]{:S(2)}) copy-start(f32[2,8,256]{2,1,0:T(8,128)} %get-tuple-element.5) | copy-start | bytes 49156
  157.1 36.2 %collective-permute-start.7 = (f32[8,4,32,256]{3,2,1,0:T(8,128)}, f32[8,4,32,256]{3,2,1,0:T(8,128)S(1)}, u32[]{:S(2)}, u32[]{:S(2)}) collective-permute-start(f32[8,4,32,256]{3,2,1,0:T(8,128)} %bitcast.1), channel_id=1, source_target_pairs={{0,184},{8,192},{16,200},{24,208},{32,216},{40,224},{48,232},{56,2... | collective-permute-start | bytes 3145736 | tf_op jit(solution)/shard_map/ppermute | solution.py:17
  157.1 47.4 %collective-permute-start.6 = (f32[8,4,32,256]{3,2,1,0:T(8,128)}, f32[8,4,32,256]{3,2,1,0:T(8,128)S(1)}, u32[]{:S(2)}, u32[]{:S(2)}) collective-permute-start(f32[8,4,32,256]{3,2,1,0:T(8,128)} %bitcast.2), channel_id=1, source_target_pairs={{0,200},{8,208},{16,216},{24,224},{32,232},{40,240},{48,248},{56,0... | collective-permute-start | bytes 3145736 | tf_op jit(solution)/shard_map/ppermute | solution.py:17
  160.1 44.4 %collective-permute-start.5 = (f32[8,4,32,256]{3,2,1,0:T(8,128)}, f32[8,4,32,256]{3,2,1,0:T(8,128)S(1)}, u32[]{:S(2)}, u32[]{:S(2)}) collective-permute-start(f32[8,4,32,256]{3,2,1,0:T(8,128)} %bitcast.3), channel_id=1, source_target_pairs={{0,56},{8,64},{16,72},{24,80},{32,88},{40,96},{48,104},{56,112},{6... | collective-permute-start | bytes 3145736 | tf_op jit(solution)/shard_map/ppermute | solution.py:17
  160.2 47.9 %collective-permute-start.4 = (f32[8,4,32,256]{3,2,1,0:T(8,128)}, f32[8,4,32,256]{3,2,1,0:T(8,128)S(1)}, u32[]{:S(2)}, u32[]{:S(2)}) collective-permute-start(f32[8,4,32,256]{3,2,1,0:T(8,128)} %bitcast.4), channel_id=1, source_target_pairs={{0,72},{8,80},{16,88},{24,96},{32,104},{40,112},{48,120},{56,128},... | collective-permute-start | bytes 3145736 | tf_op jit(solution)/shard_map/ppermute | solution.py:17
  208.1 2.5 copy-start.1
  210.6 1.2 copy-start.3
  222.0 72.9 %all-to-all-start.1 = ((f32[8,4,32,256]{3,2,1,0:T(8,128)}), f32[8,4,32,256]{3,2,1,0:T(8,128)S(1)}, u32[]{:S(2)}, u32[]{:S(2)}) async-start(f32[8,4,32,256]{3,2,1,0:T(8,128)} %shard_map.81), calls=%async_computation.1 | async-start | bytes 2097152 | tf_op jit(solution)/shard_map/all_to_all | solution.py:238
  226.2 21.9 %collective-permute-start.8 = (f32[2,8,256]{2,1,0:T(8,128)S(1)}, f32[2,8,256]{2,1,0:T(8,128)S(1)}, u32[]{:S(2)}, u32[]{:S(2)}) collective-permute-start(f32[2,8,256]{2,1,0:T(8,128)S(1)} %copy-done.7), channel_id=1, source_target_pairs={{0,1},{1,2},{2,3},{3,4},{4,5},{5,6},{6,7},{7,0},{8,9},{9,10},{10,1... | collective-permute-start | bytes 49160 | tf_op jit(solution)/shard_map/ppermute | solution.py:17
  248.1 7.3 %collective-permute-start.9 = (f32[2,8,256]{2,1,0:T(8,128)S(1)}, f32[2,8,256]{2,1,0:T(8,128)S(1)}, u32[]{:S(2)}, u32[]{:S(2)}) collective-permute-start(f32[2,8,256]{2,1,0:T(8,128)S(1)} %add.24), channel_id=1, source_target_pairs={{0,2},{1,3},{2,4},{3,5},{4,6},{5,7},{6,0},{7,1},{8,10},{9,11},{10,... | collective-permute-start | bytes 49160 | tf_op jit(solution)/shard_map/ppermute | solution.py:17
  255.4 9.2 %collective-permute-start.10 = (f32[2,8,256]{2,1,0:T(8,128)S(1)}, f32[2,8,256]{2,1,0:T(8,128)S(1)}, u32[]{:S(2)}, u32[]{:S(2)}) collective-permute-start(f32[2,8,256]{2,1,0:T(8,128)S(1)} %add.25), channel_id=1, source_target_pairs={{0,4},{1,5},{2,6},{3,7},{4,0},{5,1},{6,2},{7,3},{8,12},{9,13},{10,... | collective-permute-start | bytes 49160 | tf_op jit(solution)/shard_map/ppermute | solution.py:17
  264.6 5.3 %collective-permute-start.11 = (f32[2,8,256]{2,1,0:T(8,128)S(1)}, f32[2,8,256]{2,1,0:T(8,128)S(1)}, u32[]{:S(2)}, u32[]{:S(2)}) collective-permute-start(f32[2,8,256]{2,1,0:T(8,128)S(1)} %add.26), channel_id=1, source_target_pairs={{0,8},{8,16},{16,24},{24,32},{32,40},{40,48},{48,56},{56,64},{64,7... | collective-permute-start | bytes 49160 | tf_op jit(solution)/shard_map/ppermute | solution.py:17
  269.9 6.0 %collective-permute-start.12 = (f32[2,8,256]{2,1,0:T(8,128)S(1)}, f32[2,8,256]{2,1,0:T(8,128)S(1)}, u32[]{:S(2)}, u32[]{:S(2)}) collective-permute-start(f32[2,8,256]{2,1,0:T(8,128)S(1)} %add.27), channel_id=1, source_target_pairs={{0,16},{8,24},{16,32},{24,40},{32,48},{40,56},{48,64},{56,72},{64,... | collective-permute-start | bytes 49160 | tf_op jit(solution)/shard_map/ppermute | solution.py:17
  275.9 6.1 %collective-permute-start.13 = (f32[2,8,256]{2,1,0:T(8,128)S(1)}, f32[2,8,256]{2,1,0:T(8,128)S(1)}, u32[]{:S(2)}, u32[]{:S(2)}) collective-permute-start(f32[2,8,256]{2,1,0:T(8,128)S(1)} %add.28), channel_id=1, source_target_pairs={{0,32},{8,40},{16,48},{24,56},{32,64},{40,72},{48,80},{56,88},{64,... | collective-permute-start | bytes 49160 | tf_op jit(solution)/shard_map/ppermute | solution.py:17
  282.1 7.0 %collective-permute-start.14 = (f32[2,8,256]{2,1,0:T(8,128)S(1)}, f32[2,8,256]{2,1,0:T(8,128)S(1)}, u32[]{:S(2)}, u32[]{:S(2)}) collective-permute-start(f32[2,8,256]{2,1,0:T(8,128)S(1)} %add.29), channel_id=1, source_target_pairs={{0,64},{8,72},{16,80},{24,88},{32,96},{40,104},{48,112},{56,120},{... | collective-permute-start | bytes 49160 | tf_op jit(solution)/shard_map/ppermute | solution.py:17
  289.1 5.2 %collective-permute-start.15 = (f32[2,8,256]{2,1,0:T(8,128)S(1)}, f32[2,8,256]{2,1,0:T(8,128)S(1)}, u32[]{:S(2)}, u32[]{:S(2)}) collective-permute-start(f32[2,8,256]{2,1,0:T(8,128)S(1)} %add.30), channel_id=1, source_target_pairs={{0,128},{8,136},{16,144},{24,152},{32,160},{40,168},{48,176},{56,1... | collective-permute-start | bytes 49160 | tf_op jit(solution)/shard_map/ppermute | solution.py:17
  294.9 1.0 copy-start.6
Sparse Core Ops, SparseCore 0:
  123.7 33.4 all-gather.2

commit v2 on v0

v2 whole, which is shorter than its diff:
```python
import functools
import jax
import jax.numpy as jnp
from jax import lax
from jax.experimental import pallas as pl
from jax.experimental.pallas import tpu as pltpu
from jax.sharding import PartitionSpec as P

number_steps = (0, 1, 1, -1, -1)
spin_steps = (0, 1, -1, 1, -1)
SPINS = 8
GROUPS = ((0, 1, 4), (2, 3))
SOURCE, LIVE, COUNT, ORDER, PICK, META = 0, 32, 64, 72, 104, 136
TERMS_MAX = 16
TILE = 8
SMEM = pl.BlockSpec(memory_space=pltpu.SMEM)
VMEM = pl.BlockSpec(memory_space=pltpu.VMEM)
ANY = pl.BlockSpec(memory_space=pl.ANY)


def distance_of(kind):
    return SPINS * number_steps[kind] + spin_steps[kind]


def passed_along(value, axis, by):
    count = lax.axis_size(axis)
    return lax.ppermute(value, axis, [(i, (i + by) % count) for i in range(count)])


def plan_kernel(sec_dev, charges_ref, term_ref, meta_ref):
    devices = charges_ref.shape[1] // sec_dev
    here = lax.axis_index("sec")
    for kind in range(5):
        sender = lax.rem(here + (devices - distance_of(kind) % devices), devices)
        for slot in range(sec_dev):
            number = charges_ref[0, here * sec_dev + slot] - number_steps[kind]
            spin = charges_ref[1, here * sec_dev + slot] - spin_steps[kind]
            found, live = jnp.int32(0), jnp.int32(0)
            for other in range(sec_dev):
                same = (charges_ref[0, sender * sec_dev + other] == number) & (
                    charges_ref[1, sender * sec_dev + other] == spin
                )
                found = jnp.where(same, other, found)
                live = jnp.where(same, 1, live)
            meta_ref[SOURCE + kind * sec_dev + slot] = found
            meta_ref[LIVE + kind * sec_dev + slot] = live
    counts = [jnp.int32(0) for _ in GROUPS]
    for term in range(term_ref.shape[0]):
        kind = term_ref[term]
        for g, group in enumerate(GROUPS):
            inside, pick = kind == group[0], jnp.int32(0)
            for place, member in enumerate(group[1:], 1):
                inside = inside | (kind == member)
                pick = jnp.where(kind == member, place, pick)
            at = counts[g]
            keep_order = meta_ref[ORDER + g * TERMS_MAX + at]
            keep_pick = meta_ref[PICK + g * TERMS_MAX + at]
            meta_ref[ORDER + g * TERMS_MAX + at] = jnp.where(inside, term, keep_order)
            meta_ref[PICK + g * TERMS_MAX + at] = jnp.where(inside, pick, keep_pick)
            counts[g] = jnp.where(inside, at + 1, at)
    for g in range(len(GROUPS)):
        meta_ref[COUNT + g] = counts[g]


def make_plan(charges, term_class, sec_dev):
    return pl.pallas_call(
        functools.partial(plan_kernel, sec_dev),
        out_shape=jax.ShapeDtypeStruct((META,), jnp.int32),
        in_specs=[SMEM] * 2,
        out_specs=SMEM,
    )(charges.T, term_class)


def live_area(shape, first_row, rows, cols):
    row = lax.broadcasted_iota(jnp.int32, shape, len(shape) - 2) + first_row
    col = lax.broadcasted_iota(jnp.int32, shape, len(shape) - 1)
    return (row < rows) & (col < cols)


def mask_kernel(dims_ref, block_ref, out_ref, own_ref):
    planes = out_ref.shape[0]
    sec_dev, size, _ = block_ref.shape
    share = size // planes
    for slot in range(sec_dev):
        live = live_area((size, size), 0, dims_ref[0, slot], dims_ref[1, slot])
        masked = jnp.where(live, block_ref[slot], 0.0).reshape(planes, share, size)
        out_ref[:, slot * share : (slot + 1) * share, :] = masked
    own_ref[...] = out_ref[lax.axis_index("mpo")]


def mask_blocks(sector_dims, wavefunction, planes):
    sec_dev, size, _ = wavefunction.shape
    rows = sec_dev * size // planes
    return pl.pallas_call(
        mask_kernel,
        out_shape=(
            jax.ShapeDtypeStruct((planes, rows, size), jnp.float32),
            jax.ShapeDtypeStruct((rows, size), jnp.float32),
        ),
        in_specs=[SMEM, VMEM],
        out_specs=(VMEM, VMEM),
    )(sector_dims.T, wavefunction)


def split(value):
    high = value.astype(jnp.bfloat16)
    return high, (value - high.astype(jnp.float32)).astype(jnp.bfloat16)


def product(a, b, contract):
    dims = (((1,), (contract,)), ((), ()))
    dot = functools.partial(lax.dot_general, dimension_numbers=dims, preferred_element_type=jnp.float32)
    return dot(a[0], b[0]) + (dot(a[0], b[1]) + dot(a[1], b[0]))


def terms_kernel(group, sec_dev, meta_ref, *refs):
    kinds = GROUPS[group]
    inputs, (out_ref, high_ref, low_ref, left_buf, right_buf, sems) = refs[:-6], refs[-6:]
    left_ref, right_ref = inputs[:2]
    count = meta_ref[COUNT + group]
    size = left_ref.shape[-1]
    share = size // out_ref.shape[0]
    rows = sec_dev * share

    def copies(at):
        term = meta_ref[ORDER + group * TERMS_MAX + at]
        return (
            pltpu.make_async_copy(left_ref.at[term], left_buf.at[at], sems.at[0, at]),
            pltpu.make_async_copy(right_ref.at[term], right_buf.at[at], sems.at[1, at]),
        )

    @pl.loop(0, count)
    def _(at):
        for copy in copies(at):
            copy.start()

    for place, kind in enumerate(kinds):
        for slot in range(sec_dev):
            found = pl.multiple_of(meta_ref[SOURCE + kind * sec_dev + slot] * share, share)
            live = meta_ref[LIVE + kind * sec_dev + slot] != 0
            if group == 0:
                block = inputs[2 + place][:, pl.ds(found, share), :]
            else:
                block = inputs[2][:, place, pl.ds(found, share), :]
            high, low = split(jnp.where(live, block.reshape(size, size), 0.0))
            high_ref[place, slot] = high
            low_ref[place, slot] = low
    if group == 0:
        out_ref[...] = jnp.zeros_like(out_ref)
    else:
        out_ref[:, :rows, :] = inputs[3][...]

    @pl.loop(0, count)
    def _(at):
        for copy in copies(at):
            copy.wait()
        place = meta_ref[PICK + group * TERMS_MAX + at]
        for slot in range(sec_dev):
            source = high_ref[place, slot], low_ref[place, slot]
            middle = product(split(left_buf[at, slot]), source, 0)
            part = product(split(middle), split(right_buf[at, slot]), 1)
            out_ref[:, slot * share : (slot + 1) * share, :] += part.reshape(-1, share, size)

    if group == 1 and out_ref.shape[1] > rows:
        sums = inputs[4][...] + inputs[5][...]
        out_ref[:, rows:, :] = jnp.broadcast_to(sums[None], (out_ref.shape[0],) + sums.shape)


def apply_terms(group, meta, sources, left_env, right_env, so_far=(), sums=()):
    terms, sec_dev, size, _ = left_env.shape
    planes = sources[0].shape[0]
    rows = sec_dev * size // planes + (TILE if sums else 0)
    others = [*sources, *so_far, *sums]
    kinds = len(GROUPS[group])
    return pl.pallas_call(
        functools.partial(terms_kernel, group, sec_dev),
        out_shape=jax.ShapeDtypeStruct((planes, rows, size), jnp.float32),
        in_specs=[SMEM, ANY, ANY] + [VMEM] * len(others),
        out_specs=VMEM,
        scratch_shapes=[
            pltpu.VMEM((kinds, sec_dev, size, size), jnp.bfloat16),
            pltpu.VMEM((kinds, sec_dev, size, size), jnp.bfloat16),
            pltpu.VMEM((terms, sec_dev, size, size), jnp.float32),
            pltpu.VMEM((terms, sec_dev, size, size), jnp.float32),
            pltpu.SemaphoreType.DMA((2, terms)),
        ],
        compiler_params=pltpu.CompilerParams(vmem_limit_bytes=36 * 2**20),
        cost_estimate=pl.CostEstimate(
            flops=sec_dev * terms * 6 * size**3, bytes_accessed=4 * sec_dev * size * size * (terms + 4), transcendentals=0
        ),
    )(meta, left_env, right_env, *others)


def folded(value):
    while value.shape[0] > TILE:
        half = value.shape[0] // 2
        value = value[:half] + value[half:]
    return value


def sum_kernel(dims_ref, parts_ref, masked_ref, sigma_ref, payload_ref):
    planes, rows, size = parts_ref.shape
    sec_dev = dims_ref.shape[1]
    share = rows // sec_dev
    first_row = lax.axis_index("mpo") * share
    products, squares = [], []
    for slot in range(sec_dev):
        here = slice(slot * share, (slot + 1) * share)
        total = jnp.sum(parts_ref[:, here, :], axis=0)
        live = live_area(total.shape, first_row, dims_ref[0, slot], dims_ref[1, slot])
        sigma = jnp.where(live, total, 0.0)
        masked = masked_ref[here, :]
        sigma_ref[here, :] = sigma
        payload_ref[:, here, :] = jnp.broadcast_to(sigma[None], (planes, share, size))
        products.append(folded(masked * sigma))
        squares.append(folded(masked * masked))
    half = size // 2
    both = [sum(x[:, :half] + x[:, half:] for x in values) for values in (products, squares)]
    sums = jnp.concatenate(both, axis=1)
    payload_ref[:, rows:, :] = jnp.broadcast_to(sums[None], (planes, TILE, size))


def sum_parts(sector_dims, parts, masked):
    planes, rows, size = parts.shape
    return pl.pallas_call(
        sum_kernel,
        out_shape=(
            jax.ShapeDtypeStruct((rows, size), jnp.float32),
            jax.ShapeDtypeStruct((planes, rows + TILE, size), jnp.float32),
        ),
        in_specs=[SMEM, VMEM, VMEM],
        out_specs=(VMEM, VMEM),
    )(sector_dims.T, parts, masked)


def tile_kernel(one_ref, other_ref, sums_ref):
    rows = one_ref.shape[1] - TILE
    sums_ref[...] = jnp.sum(one_ref[:, rows:, :] + other_ref[:, rows:, :], axis=0)


def add_tiles(one, other):
    planes, rows, size = one.shape
    return pl.pallas_call(
        tile_kernel,
        out_shape=jax.ShapeDtypeStruct((TILE, size), jnp.float32),
        in_specs=[VMEM, VMEM],
        out_specs=VMEM,
    )(one, other)


def final_kernel(dims_ref, parts_ref, sigma_ref, masked_ref, residual_ref, applied_ref):
    sec_dev, share, size = residual_ref.shape
    first_row = lax.axis_index("mpo") * share
    sums = jnp.sum(parts_ref[:, sec_dev * share :, :], axis=0)
    half = size // 2
    quotient = jnp.sum(sums[:, :half], keepdims=True) / jnp.sum(sums[:, half:], keepdims=True)
    for slot in range(sec_dev):
        here = slice(slot * share, (slot + 1) * share)
        total = jnp.sum(parts_ref[:, here, :], axis=0)
        live = live_area(total.shape, first_row, dims_ref[0, slot], dims_ref[1, slot])
        sigma = sigma_ref[here, :]
        residual_ref[slot] = sigma - quotient * masked_ref[here, :]
        applied_ref[slot] = jnp.where(live, total, 0.0) - quotient * sigma


def finish(sector_dims, parts, sigma, masked):
    sec_dev = sector_dims.shape[0]
    rows, size = sigma.shape
    return pl.pallas_call(
        final_kernel,
        out_shape=(jax.ShapeDtypeStruct((sec_dev, rows // sec_dev, size), jnp.float32),) * 2,
        in_specs=[SMEM, VMEM, VMEM, VMEM],
        out_specs=(VMEM, VMEM),
    )(sector_dims.T, parts, sigma, masked)


def spread(sums):
    devices, planes = lax.axis_size("sec"), lax.axis_size("mpo")
    step = devices // planes
    return tuple(
        lax.ppermute(
            sums,
            ("sec", "mpo"),
            [
                (((i + step * m + more) % devices) * planes + m, i * planes + m)
                for i in range(devices)
                for m in range(planes)
            ],
        )
        for more in (0, 1)
    )


def gathered(share):
    pair = jnp.stack([passed_along(share, "sec", distance_of(kind)) for kind in GROUPS[1]])
    return pair, lax.all_gather(pair, "mpo", axis=0)


def direct(blocks):
    return [blocks] + [passed_along(blocks, "sec", distance_of(kind)) for kind in GROUPS[0][1:]]


def local(wavefunction, left_env, right_env, sector_dims, charges, term_class):
    planes = lax.axis_size("mpo")
    sec_dev = wavefunction.shape[0]
    masked, masked_share = mask_blocks(sector_dims, wavefunction, planes)
    pair, shares = gathered(masked_share)
    meta = make_plan(charges, term_class, sec_dev)
    first = apply_terms(0, meta, direct(masked), left_env, right_env)
    first = apply_terms(1, meta, [shares], left_env, right_env, [first])
    sigma, payload = sum_parts(sector_dims, lax.all_to_all(first, "mpo", 0, 0), masked_share)
    pair, shares = gathered(sigma)
    payload, pair = lax.optimization_barrier((payload, pair))
    sources = direct(lax.all_to_all(payload, "mpo", 0, 0))
    sums = spread(add_tiles(sources[1], sources[2]))
    second = apply_terms(0, meta, sources, left_env, right_env)
    second = apply_terms(1, meta, [shares], left_env, right_env, [second], sums)
    return finish(sector_dims, lax.all_to_all(second, "mpo", 0, 0), sigma, masked_share)


def solution(mesh):
    placed = (
        P("sec", None, None),
        P("mpo", "sec", None, None),
        P("mpo", "sec", None, None),
        P("sec", None),
        P(),
        P("mpo"),
    )
    return jax.shard_map(
        local,
        mesh=mesh,
        in_specs=placed,
        out_specs=(P("sec", "mpo", None), P("sec", "mpo", None)),
        check_vma=False,
    )
```

time: 459 us -> 285 us (0.62)
  waiting for transfers between devices: 232 us -> 61 us
  matrix products: 76.1 us -> 0 us
  blocking collectives: 53.6 us -> 113 us
  Pallas kernels: 0 us -> 29 us
  loops' own time: 19.8 us -> 0 us
  starting transfers between devices: 22.9 us -> 33.9 us
  other arithmetic: 9.71 us -> 1.45 us
    all_to_all x0 -> x3, blocking collectives: none -> 113 us  [the longest x1 40.5 us: local(): sources = direct(lax.all_to_all(payload, 'mpo', 0, 0))]
    psum x1 -> x0, waiting for transfers between devices: 84.9 us -> none  [local(): sigma_full = lax.psum(first_part, 'mpo') * live_mask]
    dot_general x28 -> x0, matrix products: 76.1 us -> none  [the longest x10 26.4 us: add_term(): jnp.einsum('irk,ick->irc', middle, right_block, precision=precise)]
    unnamed x3 -> x2, waiting for transfers between devices: 73.2 us -> 0.03 us
    psum x1 -> x0, blocking collectives: 53.6 us -> none  [local(): lax.psum((jnp.sum(masked * sigma_full), jnp.sum(masked * masked)), 'sec')]
    pallas_call x0 -> x9, Pallas kernels: none -> 29 us  [the longest x4 18.3 us: apply_terms(): pl.pallas_call(functools.partial(terms_kernel, group, sec_dev), out_shape...]
    unnamed x9 -> x34, local copies, waits for them, and re-layouts: 1.96 us -> 29.6 us
    dynamic_slice x21 -> x0, local copies, waits for them, and re-layouts: 20.9 us -> none  [the longest x10 14.1 us: add_term(): lax.dynamic_index_in_dim(stacked, term_class[term], 0, keepdims=False)]
  transfers between devices with their start and end apart: 10 -> 12, of which waited for: 6 -> 7; matrix products, arithmetic and copies ran while one was open for 5% -> 0% of each run, Pallas kernels for 0% -> 5%
where the time goes in v2:
time: 285 us; the launch traced here: 282 us
  blocking collectives  113 us (40%)
  waiting for transfers between devices  61 us (21%)
  starting transfers between devices  33.9 us (12%)
  local copies, waits for them, and re-layouts  29.6 us (10%)
  Pallas kernels  29 us (10%)
  between operations  14.1 us (5%)
    ppermute x8, waiting for transfers between devices, passed_along(): lax.ppermute(value, axis, [(i, (i + by) % count) for i in range(count)])  56.7 us
    all_to_all x1, blocking collectives, local(): sources = direct(lax.all_to_all(payload, 'mpo', 0, 0))  40.5 us
    all_to_all x1, blocking collectives, local(): lax.all_to_all(second, 'mpo', 0, 0)  38.9 us
    all_to_all x1, blocking collectives, local(): lax.all_to_all(first, 'mpo', 0, 0)  33.8 us
    unnamed x34, local copies, waits for them, and re-layouts  29.6 us
    ppermute x8, starting transfers between devices, passed_along(): lax.ppermute(value, axis, [(i, (i + by) % count) for i in range(count)])  25.7 us
    pallas_call x4, Pallas kernels, apply_terms(): pl.pallas_call(functools.partial(terms_kernel, group, sec_dev), out_shape...  18.3 us
    ppermute x2, starting transfers between devices, spread(): lax.ppermute(sums, ('sec', 'mpo'), [((i + step * m + more) % devices * pl...  8.13 us
  transfers between devices with their start and end apart: 12, of which 7 were waited for; matrix products, arithmetic and copies ran while one was open for 0% of the time, Pallas kernels for 5%

profile of v2, /device:TPU:2, one launch (start us, length us, event | category | flops | bytes accessed | tf_op | source)
XLA Modules:
  0.0 282.4 jit_solution(15301887777191327903)
XLA Ops:
  7.2 0.0 all-gather.5.cloned.1.call-start
  7.2 2.4 shard_map.78
  9.6 2.5 collective-permute-start
  12.0 0.0 collective-permute-start.1
  12.0 2.8 %collective-permute-done = f32[128,256]{1,0:T(8,128)S(1)} collective-permute-done((f32[128,256]{1,0:T(8,128)}, f32[128,256]{1,0:T(8,128)S(1)}, u32[]{:S(2)}, u32[]{:S(2)}) %collective-permute-start) | collective-permute-done | bytes 131104 | tf_op jit(solution)/shard_map/ppermute | solution.py:27
  14.9 3.0 %collective-permute-done.1 = f32[128,256]{1,0:T(8,128)S(1)} collective-permute-done((f32[128,256]{1,0:T(8,128)}, f32[128,256]{1,0:T(8,128)S(1)}, u32[]{:S(2)}, u32[]{:S(2)}) %collective-permute-start.1) | collective-permute-done | bytes 131104 | tf_op jit(solution)/shard_map/ppermute | solution.py:27
  17.8 0.7 pad_maximum_fusion
  18.6 0.0 all-gather.5.cloned.1.call-update
  18.6 0.0 all-gather.7.cloned.1.call-start
  18.6 0.6 collective-permute-start.2
  19.2 4.9 %collective-permute-start.3 = (f32[8,128,256]{2,1,0:T(8,128)}, f32[8,128,256]{2,1,0:T(8,128)S(1)}, u32[]{:S(2)}, u32[]{:S(2)}) collective-permute-start(f32[8,128,256]{2,1,0:T(8,128)} %get-tuple-element.8.refs_2_), channel_id=1, source_target_pairs={{0,184},{8,192},{16,200},{24,208},{32,216},{40,224},{48,232},{56,2... | collective-permute-start | bytes 3145736 | tf_op jit(solution)/shard_map/ppermute | solution.py:27
  24.1 1.6 shard_map.77.meta_ref
  25.6 20.3 %collective-permute-done.2.refs_3_ = f32[8,128,256]{2,1,0:T(8,128)S(1)} collective-permute-done((f32[8,128,256]{2,1,0:T(8,128)}, f32[8,128,256]{2,1,0:T(8,128)S(1)}, u32[]{:S(2)}, u32[]{:S(2)}) %collective-permute-start.2) | collective-permute-done | bytes 1048608 | tf_op jit(solution)/shard_map/ppermute | solution.py:27
  46.0 0.0 collective-permute-done.3.refs_4_
  46.0 0.0 copy-start
  46.0 2.5 copy-done
  48.5 0.0 copy-start.4
  48.5 2.5 copy-done.4
  51.0 0.0 copy-start.14
  51.0 1.2 copy-done.14
  52.3 0.0 copy-start.15
  52.3 0.7 copy-done.15
  52.9 0.0 copy-start.16
  52.9 5.3 %shard_map.79.refs_3_ = f32[8,128,256]{2,1,0:T(8,128)S(1)} custom-call(s32[136]{0:T(256)S(1)} %copy-done.15, f32[5,4,256,256]{3,2,1,0:T(8,128)S(1)} %copy-done, f32[5,4,256,256]{3,2,1,0:T(8,128)S(1)} %copy-done.4, f32[8,128,256]{2,1,0:T(8,128)S(1)} %copy-done.14, f32[8,128,256]{2,1,0:T(8,128)S(1)} %collective-permute-done.2.refs_3_, ...), custom_call_target="tpu_custom_call" | custom-call | flops 2013265920 | bytes 9437184 | tf_op jit(solution)/shard_map/pallas_call | solution.py:175
  58.2 4.2 %all-gather.5.cloned.1.call-done = f32[16,128,256]{2,1,0:T(8,128)} async-done(((f32[2,128,256]{2,1,0:T(8,128)}), f32[16,128,256]{2,1,0:T(8,128)}) %all-gather.5.cloned.1.call-update) | async-done | bytes 2097168 | tf_op jit(solution)/shard_map/all_gather | solution.py:296
  62.5 0.0 copy-done.16
  62.5 0.0 copy-start.1
  62.5 2.5 copy-done.1
  65.0 2.5 copy-done.5
  67.5 1.6 copy-done.13
  69.0 3.8 %shard_map.80 = f32[8,128,256]{2,1,0:T(8,128)S(1)} custom-call(s32[136]{0:T(256)S(1)} %copy-done.16, f32[5,4,256,256]{3,2,1,0:T(8,128)S(1)} %copy-done.1, f32[5,4,256,256]{3,2,1,0:T(8,128)S(1)} %copy-done.5, f32[8,2,128,256]{3,2,1,0:T(8,128)S(1)} %bitcast.9, f32[8,128,256]{2,1,0:T(8,128)S(1)} %shard_map.79.refs_3_), custom_call_target="tpu_custom_call" | custom-call | flops 2013265920 | bytes 9437184 | tf_op jit(solution)/shard_map/pallas_call | solution.py:175
  72.8 33.8 %all_to_all.15.parts_ref = f32[8,128,256]{2,1,0:T(8,128)} all-to-all(f32[8,128,256]{2,1,0:T(8,128)S(1)} %shard_map.80), channel_id=1, replica_groups=mesh['sec'=32,'mpo'=8] {'mpo'}, dimensions={0} | all-to-all | bytes 2097152 | tf_op jit(solution)/shard_map/all_to_all | solution.py:311
  106.6 2.4 shard_map.81
  109.0 11.1 %collective-permute-start.4 = (f32[128,256]{1,0:T(8,128)}, f32[128,256]{1,0:T(8,128)S(1)}, u32[]{:S(2)}, u32[]{:S(2)}) collective-permute-start(f32[128,256]{1,0:T(8,128)} %get-tuple-element.9.sigma_ref), channel_id=1, source_target_pairs={{0,56},{8,64},{16,72},{24,80},{32,88},{40,96},{48,104},{56,112},{6... | collective-permute-start | bytes 393224 | tf_op jit(solution)/shard_map/ppermute | solution.py:27
  120.1 0.0 collective-permute-start.5
  120.1 2.8 %collective-permute-done.4 = f32[128,256]{1,0:T(8,128)S(1)} collective-permute-done((f32[128,256]{1,0:T(8,128)}, f32[128,256]{1,0:T(8,128)S(1)}, u32[]{:S(2)}, u32[]{:S(2)}) %collective-permute-start.4) | collective-permute-done | bytes 131104 | tf_op jit(solution)/shard_map/ppermute | solution.py:27
  122.9 3.0 %collective-permute-done.5 = f32[128,256]{1,0:T(8,128)S(1)} collective-permute-done((f32[128,256]{1,0:T(8,128)}, f32[128,256]{1,0:T(8,128)S(1)}, u32[]{:S(2)}, u32[]{:S(2)}) %collective-permute-start.5) | collective-permute-done | bytes 131104 | tf_op jit(solution)/shard_map/ppermute | solution.py:27
  125.9 0.7 pad_maximum_fusion.1
  126.6 0.0 all-gather.7.cloned.1.call-update
  126.6 40.5 %all_to_all.16.refs_2_ = f32[8,136,256]{2,1,0:T(8,128)S(1)} all-to-all(f32[8,136,256]{2,1,0:T(8,128)} %get-tuple-element.11), channel_id=1, replica_groups=mesh['sec'=32,'mpo'=8] {'mpo'}, dimensions={0} | all-to-all | bytes 2228224 | tf_op jit(solution)/shard_map/all_to_all | solution.py:314
  167.1 0.0 collective-permute-start.6
  167.1 6.8 %collective-permute-start.7 = (f32[8,136,256]{2,1,0:T(8,128)S(1)}, f32[8,136,256]{2,1,0:T(8,128)S(1)}, u32[]{:S(2)}, u32[]{:S(2)}) collective-permute-start(f32[8,136,256]{2,1,0:T(8,128)S(1)} %all_to_all.16.refs_2_), channel_id=1, source_target_pairs={{0,184},{8,192},{16,200},{24,208},{32,216},{40,224},{48,232},{56,2... | collective-permute-start | bytes 3342344 | tf_op jit(solution)/shard_map/ppermute | solution.py:27
  173.9 24.8 %collective-permute-done.6.refs_3_.one_ref = f32[8,136,256]{2,1,0:T(8,128)S(1)} collective-permute-done((f32[8,136,256]{2,1,0:T(8,128)S(1)}, f32[8,136,256]{2,1,0:T(8,128)S(1)}, u32[]{:S(2)}, u32[]{:S(2)}) %collective-permute-start.6) | collective-permute-done | bytes 1114144 | tf_op jit(solution)/shard_map/ppermute | solution.py:27
  198.7 0.0 collective-permute-done.7.refs_4_.other_ref
  198.7 1.0 copy-done.8
  199.7 1.0 copy-done.10
  200.7 2.2 shard_map.83
  202.9 1.3 collective-permute-start.8
  204.2 6.8 %collective-permute-start.9 = (f32[8,256]{1,0:T(8,128)}, f32[8,256]{1,0:T(8,128)S(1)}, u32[]{:S(2)}, u32[]{:S(2)}) collective-permute-start(f32[8,256]{1,0:T(8,128)} %shard_map.83), channel_id=1, source_target_pairs={{8,0},{41,1},{74,2},{107,3},{140,4},{173,5},{206,6},{239,7},{16,8}... | collective-permute-start | bytes 24584 | tf_op jit(solution)/shard_map/ppermute | solution.py:281
  211.0 2.5 copy-done.2
  213.5 2.5 copy-done.6
  216.0 1.2 copy-done.9
  217.3 1.2 copy-done.11
  218.5 5.5 %shard_map.82.refs_3_ = f32[8,128,256]{2,1,0:T(8,128)S(1)} custom-call(s32[136]{0:T(256)S(1)} %copy-done.16, f32[5,4,256,256]{3,2,1,0:T(8,128)S(1)} %copy-done.2, f32[5,4,256,256]{3,2,1,0:T(8,128)S(1)} %copy-done.6, f32[8,136,256]{2,1,0:T(8,128)S(1)} %all_to_all.16.refs_2_, f32[8,136,256]{2,1,0:T(8,128)S(1)} %copy-done.9, f32[8,136,256]{2,1,0:T(8,128)S(1)} %copy-done.11), custom_call_target="tpu_custom_call" | custom-call | flops 2013265920 | bytes 9437184 | tf_op jit(solution)/shard_map/pallas_call | solution.py:175
  224.0 0.0 collective-permute-done.8.refs_4_
  224.0 0.0 collective-permute-done.9.refs_5_
  224.0 0.0 all-gather.7.cloned.1.call-done
  224.0 0.0 copy-start.3
  224.1 2.5 copy-done.3
  226.5 2.5 copy-done.7
  229.0 1.6 copy-done.12
  230.6 3.8 %shard_map.84 = f32[8,136,256]{2,1,0:T(8,128)S(1)} custom-call(s32[136]{0:T(256)S(1)} %copy-done.16, f32[5,4,256,256]{3,2,1,0:T(8,128)S(1)} %copy-done.3, f32[5,4,256,256]{3,2,1,0:T(8,128)S(1)} %copy-done.7, f32[8,2,128,256]{3,2,1,0:T(8,128)S(1)} %bitcast.8, f32[8,128,256]{2,1,0:T(8,128)S(1)} %shard_map.82.refs_3_, ...), custom_call_target="tpu_custom_call" | custom-call | flops 2013265920 | bytes 9437184 | tf_op jit(solution)/shard_map/pallas_call | solution.py:175
  234.4 38.9 %all_to_all.17.parts_ref = f32[8,136,256]{2,1,0:T(8,128)} all-to-all(f32[8,136,256]{2,1,0:T(8,128)S(1)} %shard_map.84), channel_id=1, replica_groups=mesh['sec'=32,'mpo'=8] {'mpo'}, dimensions={0} | all-to-all | bytes 2228224 | tf_op jit(solution)/shard_map/all_to_all | solution.py:318
  273.3 2.2 shard_map.85
  (10 shorter events, 0.0 us)
Async XLA Ops:
  7.2 55.3 %all-gather.5.cloned.1.call-start = ((), (), s32[]{:S(2)}) async-start(), calls=%async_computation.3 | async-start | bytes 2359296 | tf_op jit(solution)/shard_map/all_gather | solution.py:296
  9.6 5.3 %collective-permute-start = (f32[128,256]{1,0:T(8,128)}, f32[128,256]{1,0:T(8,128)S(1)}, u32[]{:S(2)}, u32[]{:S(2)}) collective-permute-start(f32[128,256]{1,0:T(8,128)} %get-tuple-element.7.masked_ref), channel_id=1, source_target_pairs={{0,56},{8,64},{16,72},{24,80},{32,88},{40,96},{48,104},{56,112},{6... | collective-permute-start | bytes 393224 | tf_op jit(solution)/shard_map/ppermute | solution.py:27
  12.0 5.8 %collective-permute-start.1 = (f32[128,256]{1,0:T(8,128)}, f32[128,256]{1,0:T(8,128)S(1)}, u32[]{:S(2)}, u32[]{:S(2)}) collective-permute-start(f32[128,256]{1,0:T(8,128)} %get-tuple-element.7.masked_ref), channel_id=1, source_target_pairs={{0,200},{8,208},{16,216},{24,224},{32,232},{40,240},{48,248},{56,0... | collective-permute-start | bytes 393224 | tf_op jit(solution)/shard_map/ppermute | solution.py:27
  18.6 205.5 %all-gather.7.cloned.1.call-start = ((), (), s32[]{:S(2)}) async-start(), calls=%async_computation.4 | async-start | bytes 2359296 | tf_op jit(solution)/shard_map/all_gather | solution.py:296
  18.6 27.3 %collective-permute-start.2 = (f32[8,128,256]{2,1,0:T(8,128)}, f32[8,128,256]{2,1,0:T(8,128)S(1)}, u32[]{:S(2)}, u32[]{:S(2)}) collective-permute-start(f32[8,128,256]{2,1,0:T(8,128)} %get-tuple-element.8.refs_2_), channel_id=1, source_target_pairs={{0,72},{8,80},{16,88},{24,96},{32,104},{40,112},{48,120},{56,128},... | collective-permute-start | bytes 3145736 | tf_op jit(solution)/shard_map/ppermute | solution.py:27
  19.2 26.8 %collective-permute-start.3 = (f32[8,128,256]{2,1,0:T(8,128)}, f32[8,128,256]{2,1,0:T(8,128)S(1)}, u32[]{:S(2)}, u32[]{:S(2)}) collective-permute-start(f32[8,128,256]{2,1,0:T(8,128)} %get-tuple-element.8.refs_2_), channel_id=1, source_target_pairs={{0,184},{8,192},{16,200},{24,208},{32,216},{40,224},{48,232},{56,2... | collective-permute-start | bytes 3145736 | tf_op jit(solution)/shard_map/ppermute | solution.py:27
  46.0 2.5 copy-start
  48.5 2.5 copy-start.4
  51.0 1.2 copy-start.14
  52.3 0.7 copy-start.15
  52.9 9.5 %copy-start.16 = (s32[136]{0:T(256)S(1)}, s32[136]{0:T(256)}, u32[]{:S(2)}) copy-start(s32[136]{0:T(256)} %shard_map.77.meta_ref) | copy-start | bytes 1636
  62.5 2.5 copy-start.1
  65.0 2.5 copy-start.5
  67.5 1.6 copy-start.13
  109.0 13.9 %collective-permute-start.4 = (f32[128,256]{1,0:T(8,128)}, f32[128,256]{1,0:T(8,128)S(1)}, u32[]{:S(2)}, u32[]{:S(2)}) collective-permute-start(f32[128,256]{1,0:T(8,128)} %get-tuple-element.9.sigma_ref), channel_id=1, source_target_pairs={{0,56},{8,64},{16,72},{24,80},{32,88},{40,96},{48,104},{56,112},{6... | collective-permute-start | bytes 393224 | tf_op jit(solution)/shard_map/ppermute | solution.py:27
  120.1 5.8 %collective-permute-start.5 = (f32[128,256]{1,0:T(8,128)}, f32[128,256]{1,0:T(8,128)S(1)}, u32[]{:S(2)}, u32[]{:S(2)}) collective-permute-start(f32[128,256]{1,0:T(8,128)} %get-tuple-element.9.sigma_ref), channel_id=1, source_target_pairs={{0,200},{8,208},{16,216},{24,224},{32,232},{40,240},{48,248},{56,0... | collective-permute-start | bytes 393224 | tf_op jit(solution)/shard_map/ppermute | solution.py:27
  167.1 31.5 %collective-permute-start.6 = (f32[8,136,256]{2,1,0:T(8,128)S(1)}, f32[8,136,256]{2,1,0:T(8,128)S(1)}, u32[]{:S(2)}, u32[]{:S(2)}) collective-permute-start(f32[8,136,256]{2,1,0:T(8,128)S(1)} %all_to_all.16.refs_2_), channel_id=1, source_target_pairs={{0,72},{8,80},{16,88},{24,96},{32,104},{40,112},{48,120},{56,128},... | collective-permute-start | bytes 3342344 | tf_op jit(solution)/shard_map/ppermute | solution.py:27
  167.1 31.5 %collective-permute-start.7 = (f32[8,136,256]{2,1,0:T(8,128)S(1)}, f32[8,136,256]{2,1,0:T(8,128)S(1)}, u32[]{:S(2)}, u32[]{:S(2)}) collective-permute-start(f32[8,136,256]{2,1,0:T(8,128)S(1)} %all_to_all.16.refs_2_), channel_id=1, source_target_pairs={{0,184},{8,192},{16,200},{24,208},{32,216},{40,224},{48,232},{56,2... | collective-permute-start | bytes 3342344 | tf_op jit(solution)/shard_map/ppermute | solution.py:27
  198.7 1.0 copy-start.8
  199.7 1.0 copy-start.10
  202.9 21.1 %collective-permute-start.8 = (f32[8,256]{1,0:T(8,128)}, f32[8,256]{1,0:T(8,128)S(1)}, u32[]{:S(2)}, u32[]{:S(2)}) collective-permute-start(f32[8,256]{1,0:T(8,128)} %shard_map.83), channel_id=1, source_target_pairs={{0,0},{33,1},{66,2},{99,3},{132,4},{165,5},{198,6},{231,7},{8,8},{... | collective-permute-start | bytes 24584 | tf_op jit(solution)/shard_map/ppermute | solution.py:281
  204.2 19.8 %collective-permute-start.9 = (f32[8,256]{1,0:T(8,128)}, f32[8,256]{1,0:T(8,128)S(1)}, u32[]{:S(2)}, u32[]{:S(2)}) collective-permute-start(f32[8,256]{1,0:T(8,128)} %shard_map.83), channel_id=1, source_target_pairs={{8,0},{41,1},{74,2},{107,3},{140,4},{173,5},{206,6},{239,7},{16,8}... | collective-permute-start | bytes 24584 | tf_op jit(solution)/shard_map/ppermute | solution.py:281
  211.0 2.5 copy-start.2
  213.5 2.5 copy-start.6
  216.0 1.2 copy-start.9
  217.3 1.2 copy-start.11
  224.0 2.5 copy-start.3
  226.5 2.5 copy-start.7
  229.0 1.6 copy-start.12
Sparse Core Ops, SparseCore 0:
  18.7 43.7 all-gather.4
  126.8 50.0 all-gather.6

commit v3 on v2

v3 whole, which is shorter than its diff:
```python
import functools
import jax
import jax.numpy as jnp
from jax import lax
from jax.experimental import pallas as pl
from jax.experimental.pallas import tpu as pltpu
from jax.sharding import PartitionSpec as P

number_steps = (0, 1, 1, -1, -1)
spin_steps = (0, 1, -1, 1, -1)
SPINS = 8
GROUPS = ((0, 2, 3), (1, 4), (0, 2, 3, 1, 4))
SOURCE, LIVE, COUNT, ORDER, PICK, USED, META = 0, 32, 64, 72, 104, 136, 144
TERMS_MAX = 8
TILE = 8
AHEAD = 2
SMEM = pl.BlockSpec(memory_space=pltpu.SMEM)
VMEM = pl.BlockSpec(memory_space=pltpu.VMEM)
ANY = pl.BlockSpec(memory_space=pl.ANY)
KERNEL_VMEM = 50 * 2**20
SMALL = pltpu.CompilerParams(vmem_limit_bytes=8 * 2**20)


def distance_of(kind):
    return SPINS * number_steps[kind] + spin_steps[kind]


def passed_along(value, axis, by):
    count = lax.axis_size(axis)
    return lax.ppermute(value, axis, [(i, (i + by) % count) for i in range(count)])


def plan_kernel(sec_dev, charges_ref, term_ref, meta_ref):
    devices = charges_ref.shape[1] // sec_dev
    here = lax.axis_index("sec")
    for kind in range(5):
        sender = lax.rem(here + (devices - distance_of(kind) % devices), devices)
        for slot in range(sec_dev):
            number = charges_ref[0, here * sec_dev + slot] - number_steps[kind]
            spin = charges_ref[1, here * sec_dev + slot] - spin_steps[kind]
            found, live = jnp.int32(0), jnp.int32(0)
            for other in range(sec_dev):
                same = (charges_ref[0, sender * sec_dev + other] == number) & (
                    charges_ref[1, sender * sec_dev + other] == spin
                )
                found = jnp.where(same, other, found)
                live = jnp.where(same, 1, live)
            meta_ref[SOURCE + kind * sec_dev + slot] = found
            meta_ref[LIVE + kind * sec_dev + slot] = live
    counts = [jnp.int32(0) for _ in GROUPS]
    for kind in range(5):
        used = jnp.int32(0)
        for term in range(term_ref.shape[0]):
            used = jnp.where(term_ref[term] == kind, 1, used)
        meta_ref[USED + kind] = used
    for term in range(term_ref.shape[0]):
        kind = term_ref[term]
        for g, group in enumerate(GROUPS):
            inside, pick = kind == group[0], jnp.int32(0)
            for place, member in enumerate(group[1:], 1):
                inside = inside | (kind == member)
                pick = jnp.where(kind == member, place, pick)
            at = counts[g]
            keep_order = meta_ref[ORDER + g * TERMS_MAX + at]
            keep_pick = meta_ref[PICK + g * TERMS_MAX + at]
            meta_ref[ORDER + g * TERMS_MAX + at] = jnp.where(inside, term, keep_order)
            meta_ref[PICK + g * TERMS_MAX + at] = jnp.where(inside, pick, keep_pick)
            counts[g] = jnp.where(inside, at + 1, at)
    for g in range(len(GROUPS)):
        meta_ref[COUNT + g] = counts[g]


def make_plan(charges, term_class, sec_dev):
    return pl.pallas_call(
        functools.partial(plan_kernel, sec_dev),
        out_shape=jax.ShapeDtypeStruct((META,), jnp.int32),
        in_specs=[SMEM] * 2,
        out_specs=SMEM,
        compiler_params=SMALL,
    )(charges.T, term_class)


def live_area(shape, first_row, rows, cols):
    row = lax.broadcasted_iota(jnp.int32, shape, len(shape) - 2) + first_row
    col = lax.broadcasted_iota(jnp.int32, shape, len(shape) - 1)
    return (row < rows) & (col < cols)


def mask_kernel(dims_ref, block_ref, out_ref, low_ref, own_ref, own_high_ref):
    planes = out_ref.shape[0]
    sec_dev, size, _ = block_ref.shape
    share = size // planes
    direct_rows = low_ref.shape[1]
    for slot in range(sec_dev):
        live = live_area((size, size), 0, dims_ref[0, slot], dims_ref[1, slot])
        masked = jnp.where(live, block_ref[slot], 0.0).reshape(planes, share, size)
        here = slice(slot * share, (slot + 1) * share)
        out_ref[:, here, :] = masked
        if (slot + 1) * share <= direct_rows:
            low_ref[:, here, :] = masked
    own = out_ref[lax.axis_index("mpo")]
    own_ref[...] = own
    own_high_ref[...] = own[direct_rows:]


def mask_blocks(sector_dims, wavefunction, planes):
    sec_dev, size, _ = wavefunction.shape
    rows = sec_dev * size // planes
    shapes = ((planes, rows, size), (planes, rows // 2, size), (rows, size), (rows - rows // 2, size))
    return pl.pallas_call(
        mask_kernel,
        out_shape=[jax.ShapeDtypeStruct(shape, jnp.float32) for shape in shapes],
        in_specs=[SMEM, VMEM],
        out_specs=[VMEM] * 4,
        compiler_params=SMALL,
    )(sector_dims.T, wavefunction)


def split(value):
    high = value.astype(jnp.bfloat16)
    return high, (value - high.astype(jnp.float32)).astype(jnp.bfloat16)


def product(a, b, contract):
    dims = (((1,), (contract,)), ((), ()))
    dot = functools.partial(lax.dot_general, dimension_numbers=dims, preferred_element_type=jnp.float32)
    return dot(a[0], b[0]) + (dot(a[0], b[1]) + dot(a[1], b[0]))


def folded(value):
    while value.shape[0] > TILE:
        half = value.shape[0] // 2
        value = value[:half] + value[half:]
    return value


def halved(one, other):
    half = one.shape[1] // 2
    return jnp.concatenate([x[:, :half] + x[:, half:] for x in (one, other)], axis=1)


def terms_kernel(group, sec_dev, places, turned, last, added, meta_ref, *refs):
    operands = 1 + max(at for held, _ in places for at in held) + any(part is not None for _, part in places)
    left_ref, right_ref = refs[:2]
    sources, refs = refs[2 : 2 + operands], refs[2 + operands :]
    *refs, high_ref, low_ref, left_buf, right_buf, sems = refs
    count = meta_ref[COUNT + group]
    kinds, _, size, _ = high_ref.shape

    def env_copies(at):
        term = meta_ref[ORDER + group * TERMS_MAX + at]
        return (
            pltpu.make_async_copy(left_ref.at[term], left_buf.at[at], sems.at[0, at]),
            pltpu.make_async_copy(right_ref.at[term], right_buf.at[at], sems.at[1, at]),
        )

    @pl.loop(0, count)
    def _(at):
        for copy in env_copies(at):
            copy.start()

    others, refs = refs[:added], refs[added:]
    *pieces, total_ref = refs
    total_ref[...] = others[0][...] if added > 1 else jnp.zeros_like(total_ref)
    planes, rows, _ = total_ref.shape
    share = rows // sec_dev
    plane = lax.axis_index("mpo")

    def prepare(k, kind, held, part):
        groups = [sources[at].at[i] for at in held for i in range(sources[at].shape[0])]
        direct = sec_dev if part is None else groups[0].shape[0] // share if held else 0
        for slot in range(sec_dev):
            found = meta_ref[SOURCE + kind * sec_dev + slot]
            live = meta_ref[LIVE + kind * sec_dev + slot] != 0
            first = pl.ds(pl.multiple_of(jnp.minimum(found, max(direct, 1) - 1) * share, share), share)
            second = pl.ds(pl.multiple_of(jnp.maximum(found - direct, 0) * share, share), share)
            for r in range(planes):
                to = lax.rem(plane + (planes + AHEAD - r), planes) if turned else r
                if part is None:
                    block = groups[r][first, :]
                else:
                    block = sources[-1][to, part, second, :]
                    if direct:
                        block = jnp.where(found < direct, groups[r][first, :], block)
                high, low = split(jnp.where(live, block, 0.0))
                to = pl.ds(pl.multiple_of(to * share, share), share)
                high_ref[k, slot, to, :] = high
                low_ref[k, slot, to, :] = low

    for k, (held, part) in enumerate(places):
        kind = GROUPS[group][k]
        pl.when(meta_ref[USED + kind] != 0)(functools.partial(prepare, k, kind, held, part))

    @pl.loop(0, count)
    def _(at):
        for copy in env_copies(at):
            copy.wait()
        k = meta_ref[PICK + group * TERMS_MAX + at]
        for slot in range(sec_dev):
            middle = product(split(left_buf[at, slot]), (high_ref[k, slot], low_ref[k, slot]), 0)
            part = product(split(middle), split(right_buf[at, slot]), 1)
            total_ref[:, slot * share : (slot + 1) * share, :] += part.reshape(-1, share, size)

    if last:
        own_ref, up_ref, down_ref, far_ref, two_up_ref, two_down_ref = pieces
        if added == 1:
            sums = others[0][...]
        else:
            masked_ref = others[1]
            products = [folded(total_ref[r] * masked_ref[r]) for r in range(planes)]
            own = masked_ref[plane]
            sums = halved(sum(products), folded(own * own))
        outs = (
            (own_ref, 0), (up_ref.at[0], 1), (up_ref.at[1], 3), (down_ref.at[0], -1), (down_ref.at[1], -3),
            (far_ref, 4), (two_up_ref, 2), (two_down_ref, -2),
        )
        for out_ref, away in outs:
            out_ref[:rows, :] = total_ref[lax.rem(plane + (planes + away), planes)]
            out_ref[rows:, :] = sums


def apply_terms(group, meta, operands, places, turned, envs, others=()):
    terms, sec_dev, size, _ = envs[0].shape
    planes = sum(operands[at].shape[0] for at in places[0][0])
    rows = sec_dev * size // planes
    kinds = len(GROUPS[group])
    last = bool(others)
    total = (planes, rows, size)
    scratch = [pltpu.VMEM((kinds, sec_dev, size, size), jnp.bfloat16)] * 2
    scratch += [pltpu.VMEM(envs[0].shape, jnp.float32)] * 2
    scratch += [pltpu.SemaphoreType.DMA((2, terms))]
    if last:
        piece = (rows + TILE, size)
        outs = [piece, (2, *piece), (2, *piece), piece, piece, piece]
        scratch = [pltpu.VMEM(total, jnp.float32)] + scratch
    else:
        outs = [total]
    got = pl.pallas_call(
        functools.partial(terms_kernel, group, sec_dev, places, turned, last, len(others)),
        out_shape=[jax.ShapeDtypeStruct(shape, jnp.float32) for shape in outs],
        in_specs=[SMEM, ANY, ANY] + [VMEM] * (len(operands) + len(others)),
        out_specs=[VMEM] * len(outs),
        scratch_shapes=scratch,
        compiler_params=pltpu.CompilerParams(vmem_limit_bytes=KERNEL_VMEM),
        cost_estimate=pl.CostEstimate(
            flops=sec_dev * terms * 6 * size**3, bytes_accessed=4 * sec_dev * size * size * (terms + 4), transcendentals=0
        ),
    )(meta, *envs, *operands, *others)
    return got if last else got[0]


def middle_kernel(two_up_ref, two_down_ref, up_ref, down_ref, far_ref, sum_up_ref, sum_down_ref):
    sum_up_ref[...] = two_up_ref[...] + up_ref[1]
    sum_down_ref[...] = two_down_ref[...] + (down_ref[1] + far_ref[...])


def reduce_over_planes(pieces):
    own, up, down, far, two_up, two_down = pieces
    up = passed_along(up, "mpo", 1)
    down = passed_along(down, "mpo", -1)
    far = passed_along(far, "mpo", -2)
    shape = jax.ShapeDtypeStruct(own.shape, jnp.float32)
    sum_up, sum_down = pl.pallas_call(
        middle_kernel, out_shape=(shape, shape), in_specs=[VMEM] * 5, out_specs=(VMEM, VMEM), compiler_params=SMALL
    )(two_up, two_down, up, down, far)
    return own, up, down, passed_along(sum_up, "mpo", 2), passed_along(sum_down, "mpo", -2)


def summed(refs, here):
    own_ref, up_ref, down_ref, two_up_ref, two_down_ref = refs
    near = own_ref[here, :] + (up_ref[0, here, :] + down_ref[0, here, :])
    return near + (two_up_ref[here, :] + two_down_ref[here, :])


def sum_kernel(dims_ref, *refs):
    *parts, sigma_ref, payload_ref = refs
    rows, _ = sigma_ref.shape
    sec_dev = dims_ref.shape[1]
    share = rows // sec_dev
    first_row = lax.axis_index("mpo") * share
    for slot in range(sec_dev):
        here = slice(slot * share, (slot + 1) * share)
        total = summed(parts, here)
        live = live_area(total.shape, first_row, dims_ref[0, slot], dims_ref[1, slot])
        sigma = jnp.where(live, total, 0.0)
        sigma_ref[here, :] = sigma
        payload_ref[here, :] = sigma
    payload_ref[rows:, :] = summed(parts, slice(rows, rows + TILE))


def sum_parts(sector_dims, parts):
    rows, size = parts[0].shape
    return pl.pallas_call(
        sum_kernel,
        out_shape=(
            jax.ShapeDtypeStruct((rows - TILE, size), jnp.float32),
            jax.ShapeDtypeStruct((rows, size), jnp.float32),
        ),
        in_specs=[SMEM] + [VMEM] * 5,
        out_specs=(VMEM, VMEM),
        compiler_params=SMALL,
    )(sector_dims.T, *parts)


def pair_kernel(one_ref, other_ref, pair_ref, sums_ref):
    rows = pair_ref.shape[1]
    pair_ref[0] = one_ref[:rows, :]
    pair_ref[1] = other_ref[:rows, :]
    sums_ref[...] = one_ref[rows:, :] + other_ref[rows:, :]


def make_pair(one, other):
    rows, size = one.shape
    return pl.pallas_call(
        pair_kernel,
        out_shape=(
            jax.ShapeDtypeStruct((2, rows - TILE, size), jnp.float32),
            jax.ShapeDtypeStruct((TILE, size), jnp.float32),
        ),
        in_specs=[VMEM] * 2,
        out_specs=(VMEM, VMEM),
        compiler_params=SMALL,
    )(one, other)


def assemble_kernel(*refs):
    *pieces, full_ref = refs
    for r, piece_ref in enumerate(pieces):
        full_ref[r] = piece_ref[...]


def assemble(pieces):
    return pl.pallas_call(
        assemble_kernel,
        out_shape=jax.ShapeDtypeStruct((len(pieces), *pieces[0].shape), jnp.float32),
        in_specs=[VMEM] * len(pieces),
        out_specs=VMEM,
        compiler_params=SMALL,
    )(*pieces)


def final_kernel(dims_ref, *refs):
    parts, (sigma_ref, masked_ref, residual_ref, applied_ref) = refs[:5], refs[5:]
    sec_dev, share, size = residual_ref.shape
    first_row = lax.axis_index("mpo") * share
    sums = summed(parts, slice(sec_dev * share, sec_dev * share + TILE))
    half = size // 2
    quotient = jnp.sum(sums[:, :half], keepdims=True) / jnp.sum(sums[:, half:], keepdims=True)
    for slot in range(sec_dev):
        here = slice(slot * share, (slot + 1) * share)
        total = summed(parts, here)
        live = live_area(total.shape, first_row, dims_ref[0, slot], dims_ref[1, slot])
        sigma = sigma_ref[here, :]
        residual_ref[slot] = sigma - quotient * masked_ref[here, :]
        applied_ref[slot] = jnp.where(live, total, 0.0) - quotient * sigma


def finish(sector_dims, parts, sigma, masked):
    sec_dev = sector_dims.shape[0]
    rows, size = masked.shape
    return pl.pallas_call(
        final_kernel,
        out_shape=(jax.ShapeDtypeStruct((sec_dev, rows // sec_dev, size), jnp.float32),) * 2,
        in_specs=[SMEM] + [VMEM] * 7,
        out_specs=(VMEM, VMEM),
        compiler_params=SMALL,
    )(sector_dims.T, *parts, sigma, masked)


def spread(sums):
    devices, planes = lax.axis_size("sec"), lax.axis_size("mpo")
    step = devices // planes
    return [
        lax.ppermute(
            sums,
            ("sec", "mpo"),
            [(((i + step * m + more) % devices) * planes + m, i * planes + m) for i in range(devices) for m in range(planes)],
        )
        for more in range(step // 2)
    ]


def sent(blocks, kinds):
    return [passed_along(blocks, "sec", distance_of(kind)) for kind in kinds]


def local(wavefunction, left_env, right_env, sector_dims, charges, term_class):
    planes = lax.axis_size("mpo")
    sec_dev = wavefunction.shape[0]
    envs = (left_env, right_env)
    whole_kinds, part_kinds = GROUPS[0][1:], GROUPS[1]
    masked, low, masked_share, high_share = mask_blocks(sector_dims, wavefunction, planes)
    shares = lax.all_gather(jnp.stack(sent(high_share, part_kinds)), "mpo", axis=0)
    meta = make_plan(charges, term_class, sec_dev)
    whole, part = sent(masked, whole_kinds), sent(low, part_kinds)
    whole_places = (((0,), None), ((1,), None), ((2,), None))
    first = apply_terms(0, meta, [masked, *whole], whole_places, False, envs)
    pieces = apply_terms(1, meta, [*part, shares], (((0,), 0), ((1,), 1)), False, envs, [first, masked])
    sigma, payload = sum_parts(sector_dims, reduce_over_planes(pieces))

    pair, sums = make_pair(*sent(payload, part_kinds))
    one, back_one = passed_along(sigma, "mpo", 1), passed_along(sigma, "mpo", -1)
    two, back_two = passed_along(sigma, "mpo", 2), passed_along(sigma, "mpo", -2)
    one, back_one, two, pair = lax.optimization_barrier((one, back_one, two, pair))
    shares = lax.all_gather(pair, "mpo", axis=0)
    three, back_three = passed_along(one, "mpo", 2), passed_along(back_one, "mpo", -2)
    four = passed_along(two, "mpo", 2)
    full = assemble([back_two, back_one, sigma, one, two, three, four, back_three])
    whole = sent(full, whole_kinds)
    full, sums = lax.optimization_barrier((full, sums))
    some, others = spread(sums)

    places = (*whole_places, ((), 0), ((), 1))
    pieces = apply_terms(2, meta, [full, *whole, shares], places, True, envs, [some + others])
    return finish(sector_dims, reduce_over_planes(pieces), sigma, masked_share)


def solution(mesh):
    placed = (
        P("sec", None, None),
        P("mpo", "sec", None, None),
        P("mpo", "sec", None, None),
        P("sec", None),
        P(),
        P("mpo"),
    )
    return jax.shard_map(
        local,
        mesh=mesh,
        in_specs=placed,
        out_specs=(P("sec", "mpo", None), P("sec", "mpo", None)),
        check_vma=False,
    )
```

time: 285 us -> 206 us (0.72)
  blocking collectives: 113 us -> 0 us
  starting transfers between devices: 33.9 us -> 71.7 us
  local copies, waits for them, and re-layouts: 29.6 us -> 6.37 us
  waiting for transfers between devices: 61 us -> 82.4 us
    all_to_all x3 -> x0, blocking collectives: 113 us -> none  [the longest x1 40.5 us: local(): sources = direct(lax.all_to_all(payload, 'mpo', 0, 0))]
    ppermute x8 -> x27, starting transfers between devices: 25.7 us -> 64.9 us  [passed_along(): lax.ppermute(value, axis, [(i, (i + by) % count) for i in range(count)])]
    unnamed x34 -> x20, local copies, waits for them, and re-layouts: 29.6 us -> 6.37 us
    ppermute x8 -> x27, waiting for transfers between devices: 56.7 us -> 68.8 us  [passed_along(): lax.ppermute(value, axis, [(i, (i + by) % count) for i in range(count)])]
    all_gather x2, waiting for transfers between devices: 4.25 us -> 10.4 us  [the longest x1 6.09 us: local(): shares = lax.all_gather(pair, 'mpo', axis=0)]
    ppermute x2, waiting for transfers between devices: 0.01 us -> 3.09 us  [spread(): lax.ppermute(sums, ('sec', 'mpo'), [((i + step * m + more) % devices * pl...]
    pallas_call x7 -> x9, Pallas kernels: 25.3 us -> 24.4 us  [the longest x3 22.2 us: apply_terms(): pl.pallas_call(functools.partial(terms_kernel, group, sec_dev, places, tu...]
  transfers between devices with their start and end apart: 12 -> 31, of which waited for: 7 -> 20; matrix products, arithmetic and copies ran while one was open for 0% -> 0% of each run, Pallas kernels for 5% -> 5%
where the time goes in v3:
time: 206 us; the launch traced here: 203 us
  waiting for transfers between devices  82.4 us (40%)
  starting transfers between devices  71.7 us (35%)
  Pallas kernels  27.3 us (13%)
  between operations  14.2 us (7%)
  local copies, waits for them, and re-layouts  6.37 us (3%)
    ppermute x27, waiting for transfers between devices, passed_along(): lax.ppermute(value, axis, [(i, (i + by) % count) for i in range(count)])  68.8 us
    ppermute x27, starting transfers between devices, passed_along(): lax.ppermute(value, axis, [(i, (i + by) % count) for i in range(count)])  64.9 us
    pallas_call x3, Pallas kernels, apply_terms(): pl.pallas_call(functools.partial(terms_kernel, group, sec_dev, places, tu...  22.2 us
    ppermute x2, starting transfers between devices, spread(): lax.ppermute(sums, ('sec', 'mpo'), [((i + step * m + more) % devices * pl...  6.64 us
    unnamed x20, local copies, waits for them, and re-layouts  6.37 us
    all_gather x1, waiting for transfers between devices, local(): shares = lax.all_gather(pair, 'mpo', axis=0)  6.09 us
    all_gather x1, waiting for transfers between devices, local(): lax.all_gather(jnp.stack(sent(high_share, part_kinds)), 'mpo', axis=0)  4.31 us
  transfers between devices with their start and end apart: 31, of which 20 were waited for; matrix products, arithmetic and copies ran while one was open for 0% of the time, Pallas kernels for 5%

profile of v3, /device:TPU:2, one launch (start us, length us, event | category | flops | bytes accessed | tf_op | source)
XLA Modules:
  0.0 202.5 jit_solution(182134612774863863)
XLA Ops:
  7.2 1.2 copy-done.2
  8.4 0.7 copy-done.4
  9.1 0.7 shard_map.78
  9.8 4.1 %collective-permute-start.3 = (f32[64,256]{1,0:T(8,128)S(1)}, f32[64,256]{1,0:T(8,128)S(1)}, u32[]{:S(2)}, u32[]{:S(2)}) collective-permute-start(f32[64,256]{1,0:T(8,128)S(1)} %get-tuple-element.33), channel_id=1, source_target_pairs={{0,184},{8,192},{16,200},{24,208},{32,216},{40,224},{48,232},{56,2... | collective-permute-start | bytes 196616 | tf_op jit(solution)/shard_map/ppermute | solution.py:30
  13.9 1.9 collective-permute-done.3
  15.8 5.4 %collective-permute-done.2 = f32[64,256]{1,0:T(8,128)S(1)} collective-permute-done((f32[64,256]{1,0:T(8,128)S(1)}, f32[64,256]{1,0:T(8,128)S(1)}, u32[]{:S(2)}, u32[]{:S(2)}) %collective-permute-start.2) | collective-permute-done | bytes 65568 | tf_op jit(solution)/shard_map/ppermute | solution.py:30
  21.2 0.7 pad_maximum_fusion
  21.9 0.0 all-gather.7.cloned.1.call-start
  21.9 0.1 collective-permute-start.5
  22.0 2.9 %collective-permute-start.4 = (f32[8,128,256]{2,1,0:T(8,128)S(1)}, f32[8,128,256]{2,1,0:T(8,128)S(1)}, u32[]{:S(2)}, u32[]{:S(2)}) collective-permute-start(f32[8,128,256]{2,1,0:T(8,128)S(1)} %get-tuple-element.34.refs_2_.refs_6_), channel_id=1, source_target_pairs={{0,56},{8,64},{16,72},{24,80},{32,88},{40,96},{48,104},{56,112},{6... | collective-permute-start | bytes 3145736 | tf_op jit(solution)/shard_map/ppermute | solution.py:30
  25.0 0.8 collective-permute-start.1
  25.8 0.9 collective-permute-start
  26.7 0.7 copy-done.6
  27.4 0.7 copy-done.7
  28.1 1.5 shard_map.77.meta_ref
  29.6 16.1 %collective-permute-done.5.refs_4_ = f32[8,128,256]{2,1,0:T(8,128)S(1)} collective-permute-done((f32[8,128,256]{2,1,0:T(8,128)S(1)}, f32[8,128,256]{2,1,0:T(8,128)S(1)}, u32[]{:S(2)}, u32[]{:S(2)}) %collective-permute-start.5) | collective-permute-done | bytes 1048608 | tf_op jit(solution)/shard_map/ppermute | solution.py:30
  45.6 1.0 copy-done.9
  46.6 7.9 %shard_map.79.refs_5_ = f32[8,128,256]{2,1,0:T(8,128)S(1)} custom-call(s32[144]{0:T(256)S(1)} %shard_map.77.meta_ref, f32[5,4,256,256]{3,2,1,0:T(8,128)} %refs_0_.5, f32[5,4,256,256]{3,2,1,0:T(8,128)} %refs_1_.5, f32[8,128,256]{2,1,0:T(8,128)S(1)} %get-tuple-element.34.refs_2_.refs_6_, f32[8,128,256]{2,1,0:T(8,128)S(1)} %collective-permute-done.4.refs_3_, ...), custom_call_target="tpu_custom_call" | custom-call | flops 2013265920 | bytes 9437184 | tf_op jit(solution)/shard_map/pallas_call | solution.py:238
  54.5 0.9 copy-done.1
  55.4 0.1 collective-permute-done.1.refs_3_
  55.5 4.3 %all-gather.5.cloned.1.call-done = f32[16,64,256]{2,1,0:T(8,128)} async-done(((f32[2,64,256]{2,1,0:T(8,128)}), f32[16,64,256]{2,1,0:T(8,128)}) %all-gather.5.cloned.1.call-update) | async-done | bytes 1048592 | tf_op jit(solution)/shard_map/all_gather | solution.py:393
  59.8 1.2 copy-done.3
  61.0 4.6 %shard_map.80 = (f32[136,256]{1,0:T(8,128)S(1)}, f32[2,136,256]{2,1,0:T(8,128)S(1)}, f32[2,136,256]{2,1,0:T(8,128)S(1)}, f32[136,256]{1,0:T(8,128)S(1)}, f32[136,256]{1,0:T(8,128)S(1)}, /*index=5*/f32[136,256]{1,0:T(8,128)S(1)}) custom-call(s32[144]{0:T(256)S(1)} %shard_map.77.meta_ref, f32[5,4,256,256]{3,2,1,0:T(8,128)} %refs_0_.5, ...), custom_call_target="tpu_custom_call" | custom-call | flops 2013265920 | bytes 9437184 | tf_op jit(solution)/shard_map/pallas_call | solution.py:238
  65.6 2.6 %collective-permute-start.6 = (f32[2,136,256]{2,1,0:T(8,128)S(1)}, f32[2,136,256]{2,1,0:T(8,128)S(1)}, u32[]{:S(2)}, u32[]{:S(2)}) collective-permute-start(f32[2,136,256]{2,1,0:T(8,128)S(1)} %get-tuple-element.36), channel_id=1, source_target_pairs={{0,1},{1,2},{2,3},{3,4},{4,5},{5,6},{6,7},{7,0},{8,9},{9,10},{10,1... | collective-permute-start | bytes 835592 | tf_op jit(solution)/shard_map/ppermute | solution.py:30
  68.3 0.7 collective-permute-start.7
  69.0 3.2 %collective-permute-start.8 = (f32[136,256]{1,0:T(8,128)S(1)}, f32[136,256]{1,0:T(8,128)S(1)}, u32[]{:S(2)}, u32[]{:S(2)}) collective-permute-start(f32[136,256]{1,0:T(8,128)S(1)} %get-tuple-element.40), channel_id=1, source_target_pairs={{0,6},{1,7},{2,0},{3,1},{4,2},{5,3},{6,4},{7,5},{8,14},{9,15},{10,... | collective-permute-start | bytes 417800 | tf_op jit(solution)/shard_map/ppermute | solution.py:30
  72.2 7.3 %collective-permute-done.8.far_ref = f32[136,256]{1,0:T(8,128)S(1)} collective-permute-done((f32[136,256]{1,0:T(8,128)S(1)}, f32[136,256]{1,0:T(8,128)S(1)}, u32[]{:S(2)}, u32[]{:S(2)}) %collective-permute-start.8) | collective-permute-done | bytes 139296 | tf_op jit(solution)/shard_map/ppermute | solution.py:30
  79.5 6.8 %collective-permute-start.9 = (f32[136,256]{1,0:T(8,128)S(1)}, f32[136,256]{1,0:T(8,128)S(1)}, u32[]{:S(2)}, u32[]{:S(2)}) collective-permute-start(f32[136,256]{1,0:T(8,128)S(1)} %get-tuple-element.41), channel_id=1, source_target_pairs={{0,2},{1,3},{2,4},{3,5},{4,6},{5,7},{6,0},{7,1},{8,10},{9,11},{10,... | collective-permute-start | bytes 417800 | tf_op jit(solution)/shard_map/ppermute | solution.py:30
  86.4 2.6 %collective-permute-done.9.refs_3_ = f32[136,256]{1,0:T(8,128)S(1)} collective-permute-done((f32[136,256]{1,0:T(8,128)S(1)}, f32[136,256]{1,0:T(8,128)S(1)}, u32[]{:S(2)}, u32[]{:S(2)}) %collective-permute-start.9) | collective-permute-done | bytes 139296 | tf_op jit(solution)/shard_map/ppermute | solution.py:30
  88.9 3.9 %collective-permute-done.10.refs_4_ = f32[136,256]{1,0:T(8,128)S(1)} collective-permute-done((f32[136,256]{1,0:T(8,128)S(1)}, f32[136,256]{1,0:T(8,128)S(1)}, u32[]{:S(2)}, u32[]{:S(2)}) %collective-permute-start.10) | collective-permute-done | bytes 139296 | tf_op jit(solution)/shard_map/ppermute | solution.py:30
  92.8 0.6 shard_map.82
  93.4 6.5 %collective-permute-start.16 = (f32[136,256]{1,0:T(8,128)S(1)}, f32[136,256]{1,0:T(8,128)S(1)}, u32[]{:S(2)}, u32[]{:S(2)}) collective-permute-start(f32[136,256]{1,0:T(8,128)S(1)} %get-tuple-element.44), channel_id=1, source_target_pairs={{0,184},{8,192},{16,200},{24,208},{32,216},{40,224},{48,232},{56,2... | collective-permute-start | bytes 417800 | tf_op jit(solution)/shard_map/ppermute | solution.py:30
  100.0 1.9 collective-permute-start.14
  101.9 2.0 collective-permute-start.12
  103.9 4.2 %collective-permute-done.15.one_ref = f32[136,256]{1,0:T(8,128)S(1)} collective-permute-done((f32[136,256]{1,0:T(8,128)S(1)}, f32[136,256]{1,0:T(8,128)S(1)}, u32[]{:S(2)}, u32[]{:S(2)}) %collective-permute-start.15) | collective-permute-done | bytes 139296 | tf_op jit(solution)/shard_map/ppermute | solution.py:30
  108.1 0.7 shard_map.83
  108.8 0.2 collective-permute-done.12.refs_3_
  109.0 1.8 collective-permute-start.11
  110.8 1.6 collective-permute-start.19
  112.5 1.3 collective-permute-start.17
  113.7 2.4 %collective-permute-start.18 = (f32[128,256]{1,0:T(8,128)S(1)}, f32[128,256]{1,0:T(8,128)S(1)}, u32[]{:S(2)}, u32[]{:S(2)}) collective-permute-start(f32[128,256]{1,0:T(8,128)S(1)} %collective-permute-done.14.refs_4_), channel_id=1, source_target_pairs={{0,2},{1,3},{2,4},{3,5},{4,6},{5,7},{6,0},{7,1},{8,10},{9,11},{10,... | collective-permute-start | bytes 393224 | tf_op jit(solution)/shard_map/ppermute | solution.py:30
  116.1 0.5 collective-permute-done.11.refs_0_
  116.6 3.0 %collective-permute-done.19.refs_7_ = f32[128,256]{1,0:T(8,128)S(1)} collective-permute-done((f32[128,256]{1,0:T(8,128)S(1)}, f32[128,256]{1,0:T(8,128)S(1)}, u32[]{:S(2)}, u32[]{:S(2)}) %collective-permute-start.19) | collective-permute-done | bytes 131104 | tf_op jit(solution)/shard_map/ppermute | solution.py:30
  119.6 3.5 %collective-permute-done.17.refs_5_ = f32[128,256]{1,0:T(8,128)S(1)} collective-permute-done((f32[128,256]{1,0:T(8,128)S(1)}, f32[128,256]{1,0:T(8,128)S(1)}, u32[]{:S(2)}, u32[]{:S(2)}) %collective-permute-start.17) | collective-permute-done | bytes 131104 | tf_op jit(solution)/shard_map/ppermute | solution.py:30
  123.0 1.9 collective-permute-done.18.refs_6_
  124.9 0.1 shard_map.84.refs_2_
  125.0 0.8 collective-permute-start.21
  125.7 6.9 %collective-permute-start.20 = (f32[8,128,256]{2,1,0:T(8,128)S(1)}, f32[8,128,256]{2,1,0:T(8,128)S(1)}, u32[]{:S(2)}, u32[]{:S(2)}) collective-permute-start(f32[8,128,256]{2,1,0:T(8,128)S(1)} %shard_map.84.refs_2_), channel_id=1, source_target_pairs={{0,56},{8,64},{16,72},{24,80},{32,88},{40,96},{48,104},{56,112},{6... | collective-permute-start | bytes 3145736 | tf_op jit(solution)/shard_map/ppermute | solution.py:30
  132.7 6.0 %collective-permute-start.23 = (f32[8,256]{1,0:T(8,128)S(1)}, f32[8,256]{1,0:T(8,128)S(1)}, u32[]{:S(2)}, u32[]{:S(2)}) collective-permute-start(f32[8,256]{1,0:T(8,128)S(1)} %get-tuple-element.52), channel_id=1, source_target_pairs={{8,0},{41,1},{74,2},{107,3},{140,4},{173,5},{206,6},{239,7},{16,8}... | collective-permute-start | bytes 24584 | tf_op jit(solution)/shard_map/ppermute | solution.py:374
  138.7 0.6 collective-permute-start.22
  139.3 3.1 %collective-permute-done.23 = f32[8,256]{1,0:T(8,128)S(1)} collective-permute-done((f32[8,256]{1,0:T(8,128)S(1)}, f32[8,256]{1,0:T(8,128)S(1)}, u32[]{:S(2)}, u32[]{:S(2)}) %collective-permute-start.23) | collective-permute-done | bytes 8224 | tf_op jit(solution)/shard_map/ppermute | solution.py:374
  142.4 2.6 %collective-permute-done.21.refs_4_ = f32[8,128,256]{2,1,0:T(8,128)S(1)} collective-permute-done((f32[8,128,256]{2,1,0:T(8,128)S(1)}, f32[8,128,256]{2,1,0:T(8,128)S(1)}, u32[]{:S(2)}, u32[]{:S(2)}) %collective-permute-start.21) | collective-permute-done | bytes 1048608 | tf_op jit(solution)/shard_map/ppermute | solution.py:30
  145.1 6.1 %all-gather.7.cloned.1.call-done = f32[16,128,256]{2,1,0:T(8,128)} async-done(((f32[2,128,256]{2,1,0:T(8,128)}), f32[16,128,256]{2,1,0:T(8,128)}) %all-gather.7.cloned.1.call-update) | async-done | bytes 2097168 | tf_op jit(solution)/shard_map/all_gather | solution.py:405
  151.2 9.8 %shard_map.85 = (f32[136,256]{1,0:T(8,128)S(1)}, f32[2,136,256]{2,1,0:T(8,128)S(1)}, f32[2,136,256]{2,1,0:T(8,128)S(1)}, f32[136,256]{1,0:T(8,128)S(1)}, f32[136,256]{1,0:T(8,128)S(1)}, /*index=5*/f32[136,256]{1,0:T(8,128)S(1)}) custom-call(s32[144]{0:T(256)S(1)} %shard_map.77.meta_ref, f32[5,4,256,256]{3,2,1,0:T(8,128)} %refs_0_.5, ...), custom_call_target="tpu_custom_call" | custom-call | flops 2013265920 | bytes 9437184 | tf_op jit(solution)/shard_map/pallas_call | solution.py:238
  161.0 0.9 collective-permute-start.24
  161.8 10.3 %collective-permute-start.25 = (f32[2,136,256]{2,1,0:T(8,128)S(1)}, f32[2,136,256]{2,1,0:T(8,128)S(1)}, u32[]{:S(2)}, u32[]{:S(2)}) collective-permute-start(f32[2,136,256]{2,1,0:T(8,128)S(1)} %get-tuple-element.55), channel_id=1, source_target_pairs={{0,7},{1,0},{2,1},{3,2},{4,3},{5,4},{6,5},{7,6},{8,15},{9,8},{10,9... | collective-permute-start | bytes 835592 | tf_op jit(solution)/shard_map/ppermute | solution.py:30
  172.2 1.4 collective-permute-start.26
  173.5 9.3 %collective-permute-done.26.far_ref = f32[136,256]{1,0:T(8,128)S(1)} collective-permute-done((f32[136,256]{1,0:T(8,128)S(1)}, f32[136,256]{1,0:T(8,128)S(1)}, u32[]{:S(2)}, u32[]{:S(2)}) %collective-permute-start.26) | collective-permute-done | bytes 139296 | tf_op jit(solution)/shard_map/ppermute | solution.py:30
  182.8 0.1 shard_map.86
  182.9 4.4 %collective-permute-start.27 = (f32[136,256]{1,0:T(8,128)S(1)}, f32[136,256]{1,0:T(8,128)S(1)}, u32[]{:S(2)}, u32[]{:S(2)}) collective-permute-start(f32[136,256]{1,0:T(8,128)S(1)} %get-tuple-element.59), channel_id=1, source_target_pairs={{0,2},{1,3},{2,4},{3,5},{4,6},{5,7},{6,0},{7,1},{8,10},{9,11},{10,... | collective-permute-start | bytes 417800 | tf_op jit(solution)/shard_map/ppermute | solution.py:30
  187.3 0.5 collective-permute-start.28
  187.7 4.4 %collective-permute-done.27.refs_3_ = f32[136,256]{1,0:T(8,128)S(1)} collective-permute-done((f32[136,256]{1,0:T(8,128)S(1)}, f32[136,256]{1,0:T(8,128)S(1)}, u32[]{:S(2)}, u32[]{:S(2)}) %collective-permute-start.27) | collective-permute-done | bytes 139296 | tf_op jit(solution)/shard_map/ppermute | solution.py:30
  192.2 2.1 %collective-permute-done.28.refs_4_ = f32[136,256]{1,0:T(8,128)S(1)} collective-permute-done((f32[136,256]{1,0:T(8,128)S(1)}, f32[136,256]{1,0:T(8,128)S(1)}, u32[]{:S(2)}, u32[]{:S(2)}) %collective-permute-start.28) | collective-permute-done | bytes 139296 | tf_op jit(solution)/shard_map/ppermute | solution.py:30
  194.3 1.4 shard_map.87
  (33 shorter events, 0.2 us)
Async XLA Ops:
  7.2 52.6 %all-gather.5.cloned.1.call-start = ((), (), s32[]{:S(2)}) async-start(), calls=%async_computation | async-start | bytes 1179648 | tf_op jit(solution)/shard_map/all_gather | solution.py:393
  7.2 1.2 copy-start.2
  8.4 0.7 copy-start.4
  9.8 44.6 %copy-start = (f32[8,128,256]{2,1,0:T(8,128)}, f32[8,128,256]{2,1,0:T(8,128)S(1)}, u32[]{:S(2)}) copy-start(f32[8,128,256]{2,1,0:T(8,128)S(1)} %get-tuple-element.34.refs_2_.refs_6_) | copy-start | bytes 3145732
  9.8 6.0 %collective-permute-start.3 = (f32[64,256]{1,0:T(8,128)S(1)}, f32[64,256]{1,0:T(8,128)S(1)}, u32[]{:S(2)}, u32[]{:S(2)}) collective-permute-start(f32[64,256]{1,0:T(8,128)S(1)} %get-tuple-element.33), channel_id=1, source_target_pairs={{0,184},{8,192},{16,200},{24,208},{32,216},{40,224},{48,232},{56,2... | collective-permute-start | bytes 196616 | tf_op jit(solution)/shard_map/ppermute | solution.py:30
  13.9 7.3 %collective-permute-start.2 = (f32[64,256]{1,0:T(8,128)S(1)}, f32[64,256]{1,0:T(8,128)S(1)}, u32[]{:S(2)}, u32[]{:S(2)}) collective-permute-start(f32[64,256]{1,0:T(8,128)S(1)} %get-tuple-element.33), channel_id=1, source_target_pairs={{0,72},{8,80},{16,88},{24,96},{32,104},{40,112},{48,120},{56,128},... | collective-permute-start | bytes 196616 | tf_op jit(solution)/shard_map/ppermute | solution.py:30
  21.9 129.3 %all-gather.7.cloned.1.call-start = ((), (), s32[]{:S(2)}) async-start(), calls=%async_computation.1 | async-start | bytes 2359296 | tf_op jit(solution)/shard_map/all_gather | solution.py:405
  21.9 23.7 %collective-permute-start.5 = (f32[8,128,256]{2,1,0:T(8,128)S(1)}, f32[8,128,256]{2,1,0:T(8,128)S(1)}, u32[]{:S(2)}, u32[]{:S(2)}) collective-permute-start(f32[8,128,256]{2,1,0:T(8,128)S(1)} %get-tuple-element.34.refs_2_.refs_6_), channel_id=1, source_target_pairs={{0,200},{8,208},{16,216},{24,224},{32,232},{40,240},{48,248},{56,0... | collective-permute-start | bytes 3145736 | tf_op jit(solution)/shard_map/ppermute | solution.py:30
  22.0 23.6 %collective-permute-start.4 = (f32[8,128,256]{2,1,0:T(8,128)S(1)}, f32[8,128,256]{2,1,0:T(8,128)S(1)}, u32[]{:S(2)}, u32[]{:S(2)}) collective-permute-start(f32[8,128,256]{2,1,0:T(8,128)S(1)} %get-tuple-element.34.refs_2_.refs_6_), channel_id=1, source_target_pairs={{0,56},{8,64},{16,72},{24,80},{32,88},{40,96},{48,104},{56,112},{6... | collective-permute-start | bytes 3145736 | tf_op jit(solution)/shard_map/ppermute | solution.py:30
  25.0 30.5 %collective-permute-start.1 = (f32[8,64,256]{2,1,0:T(8,128)S(1)}, f32[8,64,256]{2,1,0:T(8,128)S(1)}, u32[]{:S(2)}, u32[]{:S(2)}) collective-permute-start(f32[8,64,256]{2,1,0:T(8,128)S(1)} %get-tuple-element.32), channel_id=1, source_target_pairs={{0,184},{8,192},{16,200},{24,208},{32,216},{40,224},{48,232},{56,2... | collective-permute-start | bytes 1572872 | tf_op jit(solution)/shard_map/ppermute | solution.py:30
  25.8 29.7 %collective-permute-start = (f32[8,64,256]{2,1,0:T(8,128)S(1)}, f32[8,64,256]{2,1,0:T(8,128)S(1)}, u32[]{:S(2)}, u32[]{:S(2)}) collective-permute-start(f32[8,64,256]{2,1,0:T(8,128)S(1)} %get-tuple-element.32), channel_id=1, source_target_pairs={{0,72},{8,80},{16,88},{24,96},{32,104},{40,112},{48,120},{56,128},... | collective-permute-start | bytes 1572872 | tf_op jit(solution)/shard_map/ppermute | solution.py:30
  26.7 0.7 copy-start.6
  27.4 0.7 copy-start.7
  45.6 1.0 copy-start.9
  54.5 1.0 copy-start.1
  59.8 1.2 copy-start.3
  61.0 31.8 %copy-start.5 = (s32[4,2]{0,1:T(2,128)S(1)}, s32[4,2]{0,1:T(2,128)}, u32[]{:S(2)}) copy-start(s32[4,2]{0,1:T(2,128)} %param.9) | copy-start | bytes 100
  65.6 13.9 %collective-permute-start.6 = (f32[2,136,256]{2,1,0:T(8,128)S(1)}, f32[2,136,256]{2,1,0:T(8,128)S(1)}, u32[]{:S(2)}, u32[]{:S(2)}) collective-permute-start(f32[2,136,256]{2,1,0:T(8,128)S(1)} %get-tuple-element.36), channel_id=1, source_target_pairs={{0,1},{1,2},{2,3},{3,4},{4,5},{5,6},{6,7},{7,0},{8,9},{9,10},{10,1... | collective-permute-start | bytes 835592 | tf_op jit(solution)/shard_map/ppermute | solution.py:30
  68.3 11.2 %collective-permute-start.7 = (f32[2,136,256]{2,1,0:T(8,128)S(1)}, f32[2,136,256]{2,1,0:T(8,128)S(1)}, u32[]{:S(2)}, u32[]{:S(2)}) collective-permute-start(f32[2,136,256]{2,1,0:T(8,128)S(1)} %get-tuple-element.37), channel_id=1, source_target_pairs={{0,7},{1,0},{2,1},{3,2},{4,3},{5,4},{6,5},{7,6},{8,15},{9,8},{10,9... | collective-permute-start | bytes 835592 | tf_op jit(solution)/shard_map/ppermute | solution.py:30
  69.0 10.5 %collective-permute-start.8 = (f32[136,256]{1,0:T(8,128)S(1)}, f32[136,256]{1,0:T(8,128)S(1)}, u32[]{:S(2)}, u32[]{:S(2)}) collective-permute-start(f32[136,256]{1,0:T(8,128)S(1)} %get-tuple-element.40), channel_id=1, source_target_pairs={{0,6},{1,7},{2,0},{3,1},{4,2},{5,3},{6,4},{7,5},{8,14},{9,15},{10,... | collective-permute-start | bytes 417800 | tf_op jit(solution)/shard_map/ppermute | solution.py:30
  79.5 9.4 %collective-permute-start.9 = (f32[136,256]{1,0:T(8,128)S(1)}, f32[136,256]{1,0:T(8,128)S(1)}, u32[]{:S(2)}, u32[]{:S(2)}) collective-permute-start(f32[136,256]{1,0:T(8,128)S(1)} %get-tuple-element.41), channel_id=1, source_target_pairs={{0,2},{1,3},{2,4},{3,5},{4,6},{5,7},{6,0},{7,1},{8,10},{9,11},{10,... | collective-permute-start | bytes 417800 | tf_op jit(solution)/shard_map/ppermute | solution.py:30
  86.3 6.5 %collective-permute-start.10 = (f32[136,256]{1,0:T(8,128)S(1)}, f32[136,256]{1,0:T(8,128)S(1)}, u32[]{:S(2)}, u32[]{:S(2)}) collective-permute-start(f32[136,256]{1,0:T(8,128)S(1)} %get-tuple-element.42), channel_id=1, source_target_pairs={{0,6},{1,7},{2,0},{3,1},{4,2},{5,3},{6,4},{7,5},{8,14},{9,15},{10,... | collective-permute-start | bytes 417800 | tf_op jit(solution)/shard_map/ppermute | solution.py:30
  93.4 10.5 %collective-permute-start.16 = (f32[136,256]{1,0:T(8,128)S(1)}, f32[136,256]{1,0:T(8,128)S(1)}, u32[]{:S(2)}, u32[]{:S(2)}) collective-permute-start(f32[136,256]{1,0:T(8,128)S(1)} %get-tuple-element.44), channel_id=1, source_target_pairs={{0,184},{8,192},{16,200},{24,208},{32,216},{40,224},{48,232},{56,2... | collective-permute-start | bytes 417800 | tf_op jit(solution)/shard_map/ppermute | solution.py:30
  100.0 8.1 %collective-permute-start.15 = (f32[136,256]{1,0:T(8,128)S(1)}, f32[136,256]{1,0:T(8,128)S(1)}, u32[]{:S(2)}, u32[]{:S(2)}) collective-permute-start(f32[136,256]{1,0:T(8,128)S(1)} %get-tuple-element.44), channel_id=1, source_target_pairs={{0,72},{8,80},{16,88},{24,96},{32,104},{40,112},{48,120},{56,128},... | collective-permute-start | bytes 417800 | tf_op jit(solution)/shard_map/ppermute | solution.py:30
  100.0 8.8 %collective-permute-start.14 = (f32[128,256]{1,0:T(8,128)S(1)}, f32[128,256]{1,0:T(8,128)S(1)}, u32[]{:S(2)}, u32[]{:S(2)}) collective-permute-start(f32[128,256]{1,0:T(8,128)S(1)} %get-tuple-element.43.refs_2_.refs_5_), channel_id=1, source_target_pairs={{0,2},{1,3},{2,4},{3,5},{4,6},{5,7},{6,0},{7,1},{8,10},{9,11},{10,... | collective-permute-start | bytes 393224 | tf_op jit(solution)/shard_map/ppermute | solution.py:30
  101.9 6.9 %collective-permute-start.13 = (f32[128,256]{1,0:T(8,128)S(1)}, f32[128,256]{1,0:T(8,128)S(1)}, u32[]{:S(2)}, u32[]{:S(2)}) collective-permute-start(f32[128,256]{1,0:T(8,128)S(1)} %get-tuple-element.43.refs_2_.refs_5_), channel_id=1, source_target_pairs={{0,7},{1,0},{2,1},{3,2},{4,3},{5,4},{6,5},{7,6},{8,15},{9,8},{10,9... | collective-permute-start | bytes 393224 | tf_op jit(solution)/shard_map/ppermute | solution.py:30
  101.9 7.1 %collective-permute-start.12 = (f32[128,256]{1,0:T(8,128)S(1)}, f32[128,256]{1,0:T(8,128)S(1)}, u32[]{:S(2)}, u32[]{:S(2)}) collective-permute-start(f32[128,256]{1,0:T(8,128)S(1)} %get-tuple-element.43.refs_2_.refs_5_), channel_id=1, source_target_pairs={{0,1},{1,2},{2,3},{3,4},{4,5},{5,6},{6,7},{7,0},{8,9},{9,10},{10,1... | collective-permute-start | bytes 393224 | tf_op jit(solution)/shard_map/ppermute | solution.py:30
  109.0 7.6 %collective-permute-start.11 = (f32[128,256]{1,0:T(8,128)S(1)}, f32[128,256]{1,0:T(8,128)S(1)}, u32[]{:S(2)}, u32[]{:S(2)}) collective-permute-start(f32[128,256]{1,0:T(8,128)S(1)} %get-tuple-element.43.refs_2_.refs_5_), channel_id=1, source_target_pairs={{0,6},{1,7},{2,0},{3,1},{4,2},{5,3},{6,4},{7,5},{8,14},{9,15},{10,... | collective-permute-start | bytes 393224 | tf_op jit(solution)/shard_map/ppermute | solution.py:30
  110.8 8.7 %collective-permute-start.19 = (f32[128,256]{1,0:T(8,128)S(1)}, f32[128,256]{1,0:T(8,128)S(1)}, u32[]{:S(2)}, u32[]{:S(2)}) collective-permute-start(f32[128,256]{1,0:T(8,128)S(1)} %collective-permute-done.13.refs_1_), channel_id=1, source_target_pairs={{0,6},{1,7},{2,0},{3,1},{4,2},{5,3},{6,4},{7,5},{8,14},{9,15},{10,... | collective-permute-start | bytes 393224 | tf_op jit(solution)/shard_map/ppermute | solution.py:30
  112.5 10.6 %collective-permute-start.17 = (f32[128,256]{1,0:T(8,128)S(1)}, f32[128,256]{1,0:T(8,128)S(1)}, u32[]{:S(2)}, u32[]{:S(2)}) collective-permute-start(f32[128,256]{1,0:T(8,128)S(1)} %collective-permute-done.12.refs_3_), channel_id=1, source_target_pairs={{0,2},{1,3},{2,4},{3,5},{4,6},{5,7},{6,0},{7,1},{8,10},{9,11},{10,... | collective-permute-start | bytes 393224 | tf_op jit(solution)/shard_map/ppermute | solution.py:30
  113.7 11.2 %collective-permute-start.18 = (f32[128,256]{1,0:T(8,128)S(1)}, f32[128,256]{1,0:T(8,128)S(1)}, u32[]{:S(2)}, u32[]{:S(2)}) collective-permute-start(f32[128,256]{1,0:T(8,128)S(1)} %collective-permute-done.14.refs_4_), channel_id=1, source_target_pairs={{0,2},{1,3},{2,4},{3,5},{4,6},{5,7},{6,0},{7,1},{8,10},{9,11},{10,... | collective-permute-start | bytes 393224 | tf_op jit(solution)/shard_map/ppermute | solution.py:30
  125.0 20.1 %collective-permute-start.21 = (f32[8,128,256]{2,1,0:T(8,128)S(1)}, f32[8,128,256]{2,1,0:T(8,128)S(1)}, u32[]{:S(2)}, u32[]{:S(2)}) collective-permute-start(f32[8,128,256]{2,1,0:T(8,128)S(1)} %shard_map.84.refs_2_), channel_id=1, source_target_pairs={{0,200},{8,208},{16,216},{24,224},{32,232},{40,240},{48,248},{56,0... | collective-permute-start | bytes 3145736 | tf_op jit(solution)/shard_map/ppermute | solution.py:30
  125.7 19.3 %collective-permute-start.20 = (f32[8,128,256]{2,1,0:T(8,128)S(1)}, f32[8,128,256]{2,1,0:T(8,128)S(1)}, u32[]{:S(2)}, u32[]{:S(2)}) collective-permute-start(f32[8,128,256]{2,1,0:T(8,128)S(1)} %shard_map.84.refs_2_), channel_id=1, source_target_pairs={{0,56},{8,64},{16,72},{24,80},{32,88},{40,96},{48,104},{56,112},{6... | collective-permute-start | bytes 3145736 | tf_op jit(solution)/shard_map/ppermute | solution.py:30
  132.7 9.7 %collective-permute-start.23 = (f32[8,256]{1,0:T(8,128)S(1)}, f32[8,256]{1,0:T(8,128)S(1)}, u32[]{:S(2)}, u32[]{:S(2)}) collective-permute-start(f32[8,256]{1,0:T(8,128)S(1)} %get-tuple-element.52), channel_id=1, source_target_pairs={{8,0},{41,1},{74,2},{107,3},{140,4},{173,5},{206,6},{239,7},{16,8}... | collective-permute-start | bytes 24584 | tf_op jit(solution)/shard_map/ppermute | solution.py:374
  138.7 3.8 %collective-permute-start.22 = (f32[8,256]{1,0:T(8,128)S(1)}, f32[8,256]{1,0:T(8,128)S(1)}, u32[]{:S(2)}, u32[]{:S(2)}) collective-permute-start(f32[8,256]{1,0:T(8,128)S(1)} %get-tuple-element.52), channel_id=1, source_target_pairs={{0,0},{33,1},{66,2},{99,3},{132,4},{165,5},{198,6},{231,7},{8,8},{... | collective-permute-start | bytes 24584 | tf_op jit(solution)/shard_map/ppermute | solution.py:374
  145.1 6.1 %copy-start.8 = (f32[8,128,256]{2,1,0:T(8,128)}, f32[8,128,256]{2,1,0:T(8,128)S(1)}, u32[]{:S(2)}) copy-start(f32[8,128,256]{2,1,0:T(8,128)S(1)} %collective-permute-done.21.refs_4_) | copy-start | bytes 3145732
  161.0 21.9 %collective-permute-start.24 = (f32[2,136,256]{2,1,0:T(8,128)S(1)}, f32[2,136,256]{2,1,0:T(8,128)S(1)}, u32[]{:S(2)}, u32[]{:S(2)}) collective-permute-start(f32[2,136,256]{2,1,0:T(8,128)S(1)} %get-tuple-element.54), channel_id=1, source_target_pairs={{0,1},{1,2},{2,3},{3,4},{4,5},{5,6},{6,7},{7,0},{8,9},{9,10},{10,1... | collective-permute-start | bytes 835592 | tf_op jit(solution)/shard_map/ppermute | solution.py:30
  161.8 21.0 %collective-permute-start.25 = (f32[2,136,256]{2,1,0:T(8,128)S(1)}, f32[2,136,256]{2,1,0:T(8,128)S(1)}, u32[]{:S(2)}, u32[]{:S(2)}) collective-permute-start(f32[2,136,256]{2,1,0:T(8,128)S(1)} %get-tuple-element.55), channel_id=1, source_target_pairs={{0,7},{1,0},{2,1},{3,2},{4,3},{5,4},{6,5},{7,6},{8,15},{9,8},{10,9... | collective-permute-start | bytes 835592 | tf_op jit(solution)/shard_map/ppermute | solution.py:30
  172.2 10.7 %collective-permute-start.26 = (f32[136,256]{1,0:T(8,128)S(1)}, f32[136,256]{1,0:T(8,128)S(1)}, u32[]{:S(2)}, u32[]{:S(2)}) collective-permute-start(f32[136,256]{1,0:T(8,128)S(1)} %get-tuple-element.58), channel_id=1, source_target_pairs={{0,6},{1,7},{2,0},{3,1},{4,2},{5,3},{6,4},{7,5},{8,14},{9,15},{10,... | collective-permute-start | bytes 417800 | tf_op jit(solution)/shard_map/ppermute | solution.py:30
  182.9 9.3 %collective-permute-start.27 = (f32[136,256]{1,0:T(8,128)S(1)}, f32[136,256]{1,0:T(8,128)S(1)}, u32[]{:S(2)}, u32[]{:S(2)}) collective-permute-start(f32[136,256]{1,0:T(8,128)S(1)} %get-tuple-element.59), channel_id=1, source_target_pairs={{0,2},{1,3},{2,4},{3,5},{4,6},{5,7},{6,0},{7,1},{8,10},{9,11},{10,... | collective-permute-start | bytes 417800 | tf_op jit(solution)/shard_map/ppermute | solution.py:30
  187.3 7.0 %collective-permute-start.28 = (f32[136,256]{1,0:T(8,128)S(1)}, f32[136,256]{1,0:T(8,128)S(1)}, u32[]{:S(2)}, u32[]{:S(2)}) collective-permute-start(f32[136,256]{1,0:T(8,128)S(1)} %get-tuple-element.60), channel_id=1, source_target_pairs={{0,6},{1,7},{2,0},{3,1},{4,2},{5,3},{6,4},{7,5},{8,14},{9,15},{10,... | collective-permute-start | bytes 417800 | tf_op jit(solution)/shard_map/ppermute | solution.py:30
Sparse Core Ops, SparseCore 0:
  22.0 37.7 all-gather.4
  109.1 41.9 all-gather.6

commit v4 on v3

--- a/solution.py
+++ b/solution.py
@@ -13,7 +13,7 @@
 SOURCE, LIVE, COUNT, ORDER, PICK, USED, META = 0, 32, 64, 72, 104, 136, 144
 TERMS_MAX = 8
 TILE = 8
-AHEAD = 2
+AHEAD = 1
 SMEM = pl.BlockSpec(memory_space=pltpu.SMEM)
 VMEM = pl.BlockSpec(memory_space=pltpu.VMEM)
 ANY = pl.BlockSpec(memory_space=pl.ANY)
@@ -399,19 +399,21 @@
     sigma, payload = sum_parts(sector_dims, reduce_over_planes(pieces))
 
     pair, sums = make_pair(*sent(payload, part_kinds))
-    one, back_one = passed_along(sigma, "mpo", 1), passed_along(sigma, "mpo", -1)
-    two, back_two = passed_along(sigma, "mpo", 2), passed_along(sigma, "mpo", -2)
+    one, back_one, two = passed_along(sigma, "mpo", 1), passed_along(sigma, "mpo", -1), passed_along(sigma, "mpo", 2)
     one, back_one, two, pair = lax.optimization_barrier((one, back_one, two, pair))
     shares = lax.all_gather(pair, "mpo", axis=0)
-    three, back_three = passed_along(one, "mpo", 2), passed_along(back_one, "mpo", -2)
-    four = passed_along(two, "mpo", 2)
-    full = assemble([back_two, back_one, sigma, one, two, three, four, back_three])
-    whole = sent(full, whole_kinds)
-    full, sums = lax.optimization_barrier((full, sums))
+    near = assemble([back_one, sigma, one, two])
+    near_whole = sent(near, whole_kinds)
+    three, four = passed_along(two, "mpo", 1), passed_along(two, "mpo", 2)
+    back_two, back_three = passed_along(back_one, "mpo", -1), passed_along(back_one, "mpo", -2)
+    far = assemble([three, four, back_three, back_two])
+    far_whole = sent(far, whole_kinds)
+    far, sums = lax.optimization_barrier((far, sums))
     some, others = spread(sums)
 
-    places = (*whole_places, ((), 0), ((), 1))
-    pieces = apply_terms(2, meta, [full, *whole, shares], places, True, envs, [some + others])
+    operands = [near, far, near_whole[0], far_whole[0], near_whole[1], far_whole[1], shares]
+    places = (((0, 1), None), ((2, 3), None), ((4, 5), None), ((), 0), ((), 1))
+    pieces = apply_terms(2, meta, operands, places, True, envs, [some + others])
     return finish(sector_dims, reduce_over_planes(pieces), sigma, masked_share)
 
 

time: 206 us -> 198 us (0.961)
  starting transfers between devices: 71.7 us -> 59.5 us
  waiting for transfers between devices: 82.4 us -> 86.3 us
    ppermute x27 -> x29, starting transfers between devices: 64.9 us -> 52.9 us  [passed_along(): lax.ppermute(value, axis, [(i, (i + by) % count) for i in range(count)])]
    ppermute x27 -> x29, waiting for transfers between devices: 68.8 us -> 62.1 us  [passed_along(): lax.ppermute(value, axis, [(i, (i + by) % count) for i in range(count)])]
    all_gather x1, waiting for transfers between devices: 6.09 us -> 12.4 us  [local(): shares = lax.all_gather(pair, 'mpo', axis=0)]
    ppermute x2, waiting for transfers between devices: 3.09 us -> 7.48 us  [spread(): lax.ppermute(sums, ('sec', 'mpo'), [((i + step * m + more) % devices * pl...]
  transfers between devices with their start and end apart: 31 -> 33, of which waited for: 20 -> 20; matrix products, arithmetic and copies ran while one was open for 0% -> 0% of each run, Pallas kernels for 5% -> 5%
where the time goes in v4:
time: 198 us; the launch traced here: 194 us
  waiting for transfers between devices  86.3 us (44%)
  starting transfers between devices  59.5 us (30%)
  Pallas kernels  27.1 us (14%)
  between operations  14.2 us (7%)
  local copies, waits for them, and re-layouts  6.39 us (3%)
    ppermute x29, waiting for transfers between devices, passed_along(): lax.ppermute(value, axis, [(i, (i + by) % count) for i in range(count)])  62.1 us
    ppermute x29, starting transfers between devices, passed_along(): lax.ppermute(value, axis, [(i, (i + by) % count) for i in range(count)])  52.9 us
    pallas_call x3, Pallas kernels, apply_terms(): pl.pallas_call(functools.partial(terms_kernel, group, sec_dev, places, tu...  22.1 us
    all_gather x1, waiting for transfers between devices, local(): shares = lax.all_gather(pair, 'mpo', axis=0)  12.4 us
    ppermute x2, waiting for transfers between devices, spread(): lax.ppermute(sums, ('sec', 'mpo'), [((i + step * m + more) % devices * pl...  7.48 us
    ppermute x2, starting transfers between devices, spread(): lax.ppermute(sums, ('sec', 'mpo'), [((i + step * m + more) % devices * pl...  6.52 us
    unnamed x20, local copies, waits for them, and re-layouts  6.39 us
    all_gather x1, waiting for transfers between devices, local(): lax.all_gather(jnp.stack(sent(high_share, part_kinds)), 'mpo', axis=0)  4.31 us
  transfers between devices with their start and end apart: 33, of which 20 were waited for; matrix products, arithmetic and copies ran while one was open for 0% of the time, Pallas kernels for 5%

profile of v4, /device:TPU:2, one launch (start us, length us, event | category | flops | bytes accessed | tf_op | source)
XLA Modules:
  0.0 194.2 jit_solution(2011560879421515179)
XLA Ops:
  7.2 1.2 copy-done.2
  8.4 0.7 copy-done.4
  9.1 0.7 shard_map.78
  9.8 4.1 %collective-permute-start.3 = (f32[64,256]{1,0:T(8,128)S(1)}, f32[64,256]{1,0:T(8,128)S(1)}, u32[]{:S(2)}, u32[]{:S(2)}) collective-permute-start(f32[64,256]{1,0:T(8,128)S(1)} %get-tuple-element.33), channel_id=1, source_target_pairs={{0,184},{8,192},{16,200},{24,208},{32,216},{40,224},{48,232},{56,2... | collective-permute-start | bytes 196616 | tf_op jit(solution)/shard_map/ppermute | solution.py:30
  13.9 1.9 collective-permute-done.3
  15.8 5.4 %collective-permute-done.2 = f32[64,256]{1,0:T(8,128)S(1)} collective-permute-done((f32[64,256]{1,0:T(8,128)S(1)}, f32[64,256]{1,0:T(8,128)S(1)}, u32[]{:S(2)}, u32[]{:S(2)}) %collective-permute-start.2) | collective-permute-done | bytes 65568 | tf_op jit(solution)/shard_map/ppermute | solution.py:30
  21.2 0.7 pad_maximum_fusion
  21.9 0.0 all-gather.7.cloned.1.call-start
  21.9 0.1 collective-permute-start.5
  22.0 2.9 %collective-permute-start.4 = (f32[8,128,256]{2,1,0:T(8,128)S(1)}, f32[8,128,256]{2,1,0:T(8,128)S(1)}, u32[]{:S(2)}, u32[]{:S(2)}) collective-permute-start(f32[8,128,256]{2,1,0:T(8,128)S(1)} %get-tuple-element.34.refs_2_.refs_6_), channel_id=1, source_target_pairs={{0,56},{8,64},{16,72},{24,80},{32,88},{40,96},{48,104},{56,112},{6... | collective-permute-start | bytes 3145736 | tf_op jit(solution)/shard_map/ppermute | solution.py:30
  25.0 0.8 collective-permute-start.1
  25.8 0.9 collective-permute-start
  26.7 0.7 copy-done.6
  27.4 0.7 copy-done.7
  28.1 1.5 shard_map.77.meta_ref
  29.6 16.1 %collective-permute-done.5.refs_4_ = f32[8,128,256]{2,1,0:T(8,128)S(1)} collective-permute-done((f32[8,128,256]{2,1,0:T(8,128)S(1)}, f32[8,128,256]{2,1,0:T(8,128)S(1)}, u32[]{:S(2)}, u32[]{:S(2)}) %collective-permute-start.5) | collective-permute-done | bytes 1048608 | tf_op jit(solution)/shard_map/ppermute | solution.py:30
  45.6 1.0 copy-done.8
  46.6 7.9 %shard_map.79.refs_5_ = f32[8,128,256]{2,1,0:T(8,128)S(1)} custom-call(s32[144]{0:T(256)S(1)} %shard_map.77.meta_ref, f32[5,4,256,256]{3,2,1,0:T(8,128)} %refs_0_.5, f32[5,4,256,256]{3,2,1,0:T(8,128)} %refs_1_.5, f32[8,128,256]{2,1,0:T(8,128)S(1)} %get-tuple-element.34.refs_2_.refs_6_, f32[8,128,256]{2,1,0:T(8,128)S(1)} %collective-permute-done.4.refs_3_, ...), custom_call_target="tpu_custom_call" | custom-call | flops 2013265920 | bytes 9437184 | tf_op jit(solution)/shard_map/pallas_call | solution.py:238
  54.5 1.0 copy-done.1
  55.4 0.1 collective-permute-done.1.refs_3_
  55.5 4.3 %all-gather.5.cloned.1.call-done = f32[16,64,256]{2,1,0:T(8,128)} async-done(((f32[2,64,256]{2,1,0:T(8,128)}), f32[16,64,256]{2,1,0:T(8,128)}) %all-gather.5.cloned.1.call-update) | async-done | bytes 1048592 | tf_op jit(solution)/shard_map/all_gather | solution.py:393
  59.8 1.2 copy-done.3
  61.0 4.6 %shard_map.80 = (f32[136,256]{1,0:T(8,128)S(1)}, f32[2,136,256]{2,1,0:T(8,128)S(1)}, f32[2,136,256]{2,1,0:T(8,128)S(1)}, f32[136,256]{1,0:T(8,128)S(1)}, f32[136,256]{1,0:T(8,128)S(1)}, /*index=5*/f32[136,256]{1,0:T(8,128)S(1)}) custom-call(s32[144]{0:T(256)S(1)} %shard_map.77.meta_ref, f32[5,4,256,256]{3,2,1,0:T(8,128)} %refs_0_.5, ...), custom_call_target="tpu_custom_call" | custom-call | flops 2013265920 | bytes 9437184 | tf_op jit(solution)/shard_map/pallas_call | solution.py:238
  65.6 5.1 %collective-permute-start.6 = (f32[2,136,256]{2,1,0:T(8,128)S(1)}, f32[2,136,256]{2,1,0:T(8,128)S(1)}, u32[]{:S(2)}, u32[]{:S(2)}) collective-permute-start(f32[2,136,256]{2,1,0:T(8,128)S(1)} %get-tuple-element.36), channel_id=1, source_target_pairs={{0,1},{1,2},{2,3},{3,4},{4,5},{5,6},{6,7},{7,0},{8,9},{9,10},{10,1... | collective-permute-start | bytes 835592 | tf_op jit(solution)/shard_map/ppermute | solution.py:30
  70.7 1.5 collective-permute-start.8
  72.2 9.1 %collective-permute-done.8.far_ref = f32[136,256]{1,0:T(8,128)S(1)} collective-permute-done((f32[136,256]{1,0:T(8,128)S(1)}, f32[136,256]{1,0:T(8,128)S(1)}, u32[]{:S(2)}, u32[]{:S(2)}) %collective-permute-start.8) | collective-permute-done | bytes 139296 | tf_op jit(solution)/shard_map/ppermute | solution.py:30
  81.3 5.0 %collective-permute-start.9 = (f32[136,256]{1,0:T(8,128)S(1)}, f32[136,256]{1,0:T(8,128)S(1)}, u32[]{:S(2)}, u32[]{:S(2)}) collective-permute-start(f32[136,256]{1,0:T(8,128)S(1)} %get-tuple-element.41), channel_id=1, source_target_pairs={{0,2},{1,3},{2,4},{3,5},{4,6},{5,7},{6,0},{7,1},{8,10},{9,11},{10,... | collective-permute-start | bytes 417800 | tf_op jit(solution)/shard_map/ppermute | solution.py:30
  86.3 3.9 %collective-permute-done.9.refs_3_ = f32[136,256]{1,0:T(8,128)S(1)} collective-permute-done((f32[136,256]{1,0:T(8,128)S(1)}, f32[136,256]{1,0:T(8,128)S(1)}, u32[]{:S(2)}, u32[]{:S(2)}) %collective-permute-start.9) | collective-permute-done | bytes 139296 | tf_op jit(solution)/shard_map/ppermute | solution.py:30
  90.2 2.5 %collective-permute-done.10.refs_4_ = f32[136,256]{1,0:T(8,128)S(1)} collective-permute-done((f32[136,256]{1,0:T(8,128)S(1)}, f32[136,256]{1,0:T(8,128)S(1)}, u32[]{:S(2)}, u32[]{:S(2)}) %collective-permute-start.10) | collective-permute-done | bytes 139296 | tf_op jit(solution)/shard_map/ppermute | solution.py:30
  92.7 0.6 shard_map.82
  93.3 4.1 %collective-permute-start.15 = (f32[136,256]{1,0:T(8,128)S(1)}, f32[136,256]{1,0:T(8,128)S(1)}, u32[]{:S(2)}, u32[]{:S(2)}) collective-permute-start(f32[136,256]{1,0:T(8,128)S(1)} %get-tuple-element.44), channel_id=1, source_target_pairs={{0,184},{8,192},{16,200},{24,208},{32,216},{40,224},{48,232},{56,2... | collective-permute-start | bytes 417800 | tf_op jit(solution)/shard_map/ppermute | solution.py:30
  97.4 4.9 %collective-permute-start.13 = (f32[128,256]{1,0:T(8,128)S(1)}, f32[128,256]{1,0:T(8,128)S(1)}, u32[]{:S(2)}, u32[]{:S(2)}) collective-permute-start(f32[128,256]{1,0:T(8,128)S(1)} %get-tuple-element.43.refs_1_.refs_5_), channel_id=1, source_target_pairs={{0,2},{1,3},{2,4},{3,5},{4,6},{5,7},{6,0},{7,1},{8,10},{9,11},{10,... | collective-permute-start | bytes 393224 | tf_op jit(solution)/shard_map/ppermute | solution.py:30
  102.3 2.0 %collective-permute-start.11 = (f32[128,256]{1,0:T(8,128)S(1)}, f32[128,256]{1,0:T(8,128)S(1)}, u32[]{:S(2)}, u32[]{:S(2)}) collective-permute-start(f32[128,256]{1,0:T(8,128)S(1)} %get-tuple-element.43.refs_1_.refs_5_), channel_id=1, source_target_pairs={{0,1},{1,2},{2,3},{3,4},{4,5},{5,6},{6,7},{7,0},{8,9},{9,10},{10,1... | collective-permute-start | bytes 393224 | tf_op jit(solution)/shard_map/ppermute | solution.py:30
  104.3 1.2 collective-permute-done.14.one_ref
  105.5 0.7 shard_map.83
  106.2 1.1 collective-permute-done.12.refs_0_
  107.2 1.2 collective-permute-done.11.refs_2_
  108.5 0.1 collective-permute-start.19
  108.6 1.8 collective-permute-start.18
  110.3 1.2 collective-permute-start.17
  111.6 1.9 collective-permute-start.16
  113.5 0.1 collective-permute-start.22
  113.6 0.7 collective-permute-done.19.refs_3_
  114.3 2.3 %collective-permute-start.20 = (f32[4,128,256]{2,1,0:T(8,128)S(1)}, f32[4,128,256]{2,1,0:T(8,128)S(1)}, u32[]{:S(2)}, u32[]{:S(2)}) collective-permute-start(f32[4,128,256]{2,1,0:T(8,128)S(1)} %shard_map.84.refs_2_), channel_id=1, source_target_pairs={{0,56},{8,64},{16,72},{24,80},{32,88},{40,96},{48,104},{56,112},{6... | collective-permute-start | bytes 1572872 | tf_op jit(solution)/shard_map/ppermute | solution.py:30
  116.6 1.0 collective-permute-done.18.refs_2_
  117.6 0.7 collective-permute-done.17.refs_1_
  118.3 1.8 collective-permute-done.16.refs_0_
  120.2 0.8 collective-permute-start.23
  121.0 2.2 %collective-permute-start.21 = (f32[4,128,256]{2,1,0:T(8,128)S(1)}, f32[4,128,256]{2,1,0:T(8,128)S(1)}, u32[]{:S(2)}, u32[]{:S(2)}) collective-permute-start(f32[4,128,256]{2,1,0:T(8,128)S(1)} %shard_map.85.refs_3_), channel_id=1, source_target_pairs={{0,56},{8,64},{16,72},{24,80},{32,88},{40,96},{48,104},{56,112},{6... | collective-permute-start | bytes 1572872 | tf_op jit(solution)/shard_map/ppermute | solution.py:30
  123.2 5.9 %collective-permute-start.25 = (f32[8,256]{1,0:T(8,128)S(1)}, f32[8,256]{1,0:T(8,128)S(1)}, u32[]{:S(2)}, u32[]{:S(2)}) collective-permute-start(f32[8,256]{1,0:T(8,128)S(1)} %get-tuple-element.52), channel_id=1, source_target_pairs={{8,0},{41,1},{74,2},{107,3},{140,4},{173,5},{206,6},{239,7},{16,8}... | collective-permute-start | bytes 24584 | tf_op jit(solution)/shard_map/ppermute | solution.py:374
  129.1 7.5 %collective-permute-done.25 = f32[8,256]{1,0:T(8,128)S(1)} collective-permute-done((f32[8,256]{1,0:T(8,128)S(1)}, f32[8,256]{1,0:T(8,128)S(1)}, u32[]{:S(2)}, u32[]{:S(2)}) %collective-permute-start.25) | collective-permute-done | bytes 8224 | tf_op jit(solution)/shard_map/ppermute | solution.py:374
  136.6 0.6 collective-permute-start.24
  137.3 12.4 %all-gather.7.cloned.1.call-done = f32[16,128,256]{2,1,0:T(8,128)} async-done(((f32[2,128,256]{2,1,0:T(8,128)}), f32[16,128,256]{2,1,0:T(8,128)}) %all-gather.7.cloned.1.call-update) | async-done | bytes 2097168 | tf_op jit(solution)/shard_map/all_gather | solution.py:404
  149.7 9.6 %shard_map.86 = (f32[136,256]{1,0:T(8,128)S(1)}, f32[2,136,256]{2,1,0:T(8,128)S(1)}, f32[2,136,256]{2,1,0:T(8,128)S(1)}, f32[136,256]{1,0:T(8,128)S(1)}, f32[136,256]{1,0:T(8,128)S(1)}, /*index=5*/f32[136,256]{1,0:T(8,128)S(1)}) custom-call(s32[144]{0:T(256)S(1)} %shard_map.77.meta_ref, f32[5,4,256,256]{3,2,1,0:T(8,128)} %refs_0_.5, ...), custom_call_target="tpu_custom_call" | custom-call | flops 2013265920 | bytes 9437184 | tf_op jit(solution)/shard_map/pallas_call | solution.py:238
  159.4 1.1 collective-permute-start.26
  160.4 4.4 %collective-permute-start.27 = (f32[2,136,256]{2,1,0:T(8,128)S(1)}, f32[2,136,256]{2,1,0:T(8,128)S(1)}, u32[]{:S(2)}, u32[]{:S(2)}) collective-permute-start(f32[2,136,256]{2,1,0:T(8,128)S(1)} %get-tuple-element.55), channel_id=1, source_target_pairs={{0,7},{1,0},{2,1},{3,2},{4,3},{5,4},{6,5},{7,6},{8,15},{9,8},{10,9... | collective-permute-start | bytes 835592 | tf_op jit(solution)/shard_map/ppermute | solution.py:30
  164.8 1.4 collective-permute-start.28
  166.2 9.5 %collective-permute-done.28.far_ref = f32[136,256]{1,0:T(8,128)S(1)} collective-permute-done((f32[136,256]{1,0:T(8,128)S(1)}, f32[136,256]{1,0:T(8,128)S(1)}, u32[]{:S(2)}, u32[]{:S(2)}) %collective-permute-start.28) | collective-permute-done | bytes 139296 | tf_op jit(solution)/shard_map/ppermute | solution.py:30
  175.7 0.1 shard_map.87
  175.8 2.8 %collective-permute-start.29 = (f32[136,256]{1,0:T(8,128)S(1)}, f32[136,256]{1,0:T(8,128)S(1)}, u32[]{:S(2)}, u32[]{:S(2)}) collective-permute-start(f32[136,256]{1,0:T(8,128)S(1)} %get-tuple-element.59), channel_id=1, source_target_pairs={{0,2},{1,3},{2,4},{3,5},{4,6},{5,7},{6,0},{7,1},{8,10},{9,11},{10,... | collective-permute-start | bytes 417800 | tf_op jit(solution)/shard_map/ppermute | solution.py:30
  178.6 1.4 collective-permute-start.30
  180.0 4.9 %collective-permute-done.29.refs_3_ = f32[136,256]{1,0:T(8,128)S(1)} collective-permute-done((f32[136,256]{1,0:T(8,128)S(1)}, f32[136,256]{1,0:T(8,128)S(1)}, u32[]{:S(2)}, u32[]{:S(2)}) %collective-permute-start.29) | collective-permute-done | bytes 139296 | tf_op jit(solution)/shard_map/ppermute | solution.py:30
  184.9 1.1 collective-permute-done.30.refs_4_
  186.0 1.4 shard_map.88
  (38 shorter events, 0.3 us)
Async XLA Ops:
  7.2 52.6 %all-gather.5.cloned.1.call-start = ((), (), s32[]{:S(2)}) async-start(), calls=%async_computation | async-start | bytes 1179648 | tf_op jit(solution)/shard_map/all_gather | solution.py:393
  7.2 1.2 copy-start.2
  8.4 0.7 copy-start.4
  9.8 44.7 %copy-start = (f32[8,128,256]{2,1,0:T(8,128)}, f32[8,128,256]{2,1,0:T(8,128)S(1)}, u32[]{:S(2)}) copy-start(f32[8,128,256]{2,1,0:T(8,128)S(1)} %get-tuple-element.34.refs_2_.refs_6_) | copy-start | bytes 3145732
  9.8 6.0 %collective-permute-start.3 = (f32[64,256]{1,0:T(8,128)S(1)}, f32[64,256]{1,0:T(8,128)S(1)}, u32[]{:S(2)}, u32[]{:S(2)}) collective-permute-start(f32[64,256]{1,0:T(8,128)S(1)} %get-tuple-element.33), channel_id=1, source_target_pairs={{0,184},{8,192},{16,200},{24,208},{32,216},{40,224},{48,232},{56,2... | collective-permute-start | bytes 196616 | tf_op jit(solution)/shard_map/ppermute | solution.py:30
  13.9 7.3 %collective-permute-start.2 = (f32[64,256]{1,0:T(8,128)S(1)}, f32[64,256]{1,0:T(8,128)S(1)}, u32[]{:S(2)}, u32[]{:S(2)}) collective-permute-start(f32[64,256]{1,0:T(8,128)S(1)} %get-tuple-element.33), channel_id=1, source_target_pairs={{0,72},{8,80},{16,88},{24,96},{32,104},{40,112},{48,120},{56,128},... | collective-permute-start | bytes 196616 | tf_op jit(solution)/shard_map/ppermute | solution.py:30
  21.9 127.8 %all-gather.7.cloned.1.call-start = ((), (), s32[]{:S(2)}) async-start(), calls=%async_computation.1 | async-start | bytes 2359296 | tf_op jit(solution)/shard_map/all_gather | solution.py:404
  21.9 23.7 %collective-permute-start.5 = (f32[8,128,256]{2,1,0:T(8,128)S(1)}, f32[8,128,256]{2,1,0:T(8,128)S(1)}, u32[]{:S(2)}, u32[]{:S(2)}) collective-permute-start(f32[8,128,256]{2,1,0:T(8,128)S(1)} %get-tuple-element.34.refs_2_.refs_6_), channel_id=1, source_target_pairs={{0,200},{8,208},{16,216},{24,224},{32,232},{40,240},{48,248},{56,0... | collective-permute-start | bytes 3145736 | tf_op jit(solution)/shard_map/ppermute | solution.py:30
  22.0 23.6 %collective-permute-start.4 = (f32[8,128,256]{2,1,0:T(8,128)S(1)}, f32[8,128,256]{2,1,0:T(8,128)S(1)}, u32[]{:S(2)}, u32[]{:S(2)}) collective-permute-start(f32[8,128,256]{2,1,0:T(8,128)S(1)} %get-tuple-element.34.refs_2_.refs_6_), channel_id=1, source_target_pairs={{0,56},{8,64},{16,72},{24,80},{32,88},{40,96},{48,104},{56,112},{6... | collective-permute-start | bytes 3145736 | tf_op jit(solution)/shard_map/ppermute | solution.py:30
  25.0 30.5 %collective-permute-start.1 = (f32[8,64,256]{2,1,0:T(8,128)S(1)}, f32[8,64,256]{2,1,0:T(8,128)S(1)}, u32[]{:S(2)}, u32[]{:S(2)}) collective-permute-start(f32[8,64,256]{2,1,0:T(8,128)S(1)} %get-tuple-element.32), channel_id=1, source_target_pairs={{0,184},{8,192},{16,200},{24,208},{32,216},{40,224},{48,232},{56,2... | collective-permute-start | bytes 1572872 | tf_op jit(solution)/shard_map/ppermute | solution.py:30
  25.8 29.7 %collective-permute-start = (f32[8,64,256]{2,1,0:T(8,128)S(1)}, f32[8,64,256]{2,1,0:T(8,128)S(1)}, u32[]{:S(2)}, u32[]{:S(2)}) collective-permute-start(f32[8,64,256]{2,1,0:T(8,128)S(1)} %get-tuple-element.32), channel_id=1, source_target_pairs={{0,72},{8,80},{16,88},{24,96},{32,104},{40,112},{48,120},{56,128},... | collective-permute-start | bytes 1572872 | tf_op jit(solution)/shard_map/ppermute | solution.py:30
  26.7 0.7 copy-start.6
  27.4 0.7 copy-start.7
  45.6 1.0 copy-start.8
  54.5 1.0 copy-start.1
  59.8 1.2 copy-start.3
  61.0 31.7 %copy-start.5 = (s32[4,2]{0,1:T(2,128)S(1)}, s32[4,2]{0,1:T(2,128)}, u32[]{:S(2)}) copy-start(s32[4,2]{0,1:T(2,128)} %param.9) | copy-start | bytes 100
  65.6 15.6 %collective-permute-start.6 = (f32[2,136,256]{2,1,0:T(8,128)S(1)}, f32[2,136,256]{2,1,0:T(8,128)S(1)}, u32[]{:S(2)}, u32[]{:S(2)}) collective-permute-start(f32[2,136,256]{2,1,0:T(8,128)S(1)} %get-tuple-element.36), channel_id=1, source_target_pairs={{0,1},{1,2},{2,3},{3,4},{4,5},{5,6},{6,7},{7,0},{8,9},{9,10},{10,1... | collective-permute-start | bytes 835592 | tf_op jit(solution)/shard_map/ppermute | solution.py:30
  70.7 10.6 %collective-permute-start.7 = (f32[2,136,256]{2,1,0:T(8,128)S(1)}, f32[2,136,256]{2,1,0:T(8,128)S(1)}, u32[]{:S(2)}, u32[]{:S(2)}) collective-permute-start(f32[2,136,256]{2,1,0:T(8,128)S(1)} %get-tuple-element.37), channel_id=1, source_target_pairs={{0,7},{1,0},{2,1},{3,2},{4,3},{5,4},{6,5},{7,6},{8,15},{9,8},{10,9... | collective-permute-start | bytes 835592 | tf_op jit(solution)/shard_map/ppermute | solution.py:30
  70.7 10.5 %collective-permute-start.8 = (f32[136,256]{1,0:T(8,128)S(1)}, f32[136,256]{1,0:T(8,128)S(1)}, u32[]{:S(2)}, u32[]{:S(2)}) collective-permute-start(f32[136,256]{1,0:T(8,128)S(1)} %get-tuple-element.40), channel_id=1, source_target_pairs={{0,6},{1,7},{2,0},{3,1},{4,2},{5,3},{6,4},{7,5},{8,14},{9,15},{10,... | collective-permute-start | bytes 417800 | tf_op jit(solution)/shard_map/ppermute | solution.py:30
  81.3 8.9 %collective-permute-start.9 = (f32[136,256]{1,0:T(8,128)S(1)}, f32[136,256]{1,0:T(8,128)S(1)}, u32[]{:S(2)}, u32[]{:S(2)}) collective-permute-start(f32[136,256]{1,0:T(8,128)S(1)} %get-tuple-element.41), channel_id=1, source_target_pairs={{0,2},{1,3},{2,4},{3,5},{4,6},{5,7},{6,0},{7,1},{8,10},{9,11},{10,... | collective-permute-start | bytes 417800 | tf_op jit(solution)/shard_map/ppermute | solution.py:30
  86.3 6.4 %collective-permute-start.10 = (f32[136,256]{1,0:T(8,128)S(1)}, f32[136,256]{1,0:T(8,128)S(1)}, u32[]{:S(2)}, u32[]{:S(2)}) collective-permute-start(f32[136,256]{1,0:T(8,128)S(1)} %get-tuple-element.42), channel_id=1, source_target_pairs={{0,6},{1,7},{2,0},{3,1},{4,2},{5,3},{6,4},{7,5},{8,14},{9,15},{10,... | collective-permute-start | bytes 417800 | tf_op jit(solution)/shard_map/ppermute | solution.py:30
  93.3 11.0 %collective-permute-start.15 = (f32[136,256]{1,0:T(8,128)S(1)}, f32[136,256]{1,0:T(8,128)S(1)}, u32[]{:S(2)}, u32[]{:S(2)}) collective-permute-start(f32[136,256]{1,0:T(8,128)S(1)} %get-tuple-element.44), channel_id=1, source_target_pairs={{0,184},{8,192},{16,200},{24,208},{32,216},{40,224},{48,232},{56,2... | collective-permute-start | bytes 417800 | tf_op jit(solution)/shard_map/ppermute | solution.py:30
  97.4 8.1 %collective-permute-start.14 = (f32[136,256]{1,0:T(8,128)S(1)}, f32[136,256]{1,0:T(8,128)S(1)}, u32[]{:S(2)}, u32[]{:S(2)}) collective-permute-start(f32[136,256]{1,0:T(8,128)S(1)} %get-tuple-element.44), channel_id=1, source_target_pairs={{0,72},{8,80},{16,88},{24,96},{32,104},{40,112},{48,120},{56,128},... | collective-permute-start | bytes 417800 | tf_op jit(solution)/shard_map/ppermute | solution.py:30
  97.4 8.8 %collective-permute-start.13 = (f32[128,256]{1,0:T(8,128)S(1)}, f32[128,256]{1,0:T(8,128)S(1)}, u32[]{:S(2)}, u32[]{:S(2)}) collective-permute-start(f32[128,256]{1,0:T(8,128)S(1)} %get-tuple-element.43.refs_1_.refs_5_), channel_id=1, source_target_pairs={{0,2},{1,3},{2,4},{3,5},{4,6},{5,7},{6,0},{7,1},{8,10},{9,11},{10,... | collective-permute-start | bytes 393224 | tf_op jit(solution)/shard_map/ppermute | solution.py:30
  102.3 5.0 %collective-permute-start.12 = (f32[128,256]{1,0:T(8,128)S(1)}, f32[128,256]{1,0:T(8,128)S(1)}, u32[]{:S(2)}, u32[]{:S(2)}) collective-permute-start(f32[128,256]{1,0:T(8,128)S(1)} %get-tuple-element.43.refs_1_.refs_5_), channel_id=1, source_target_pairs={{0,7},{1,0},{2,1},{3,2},{4,3},{5,4},{6,5},{7,6},{8,15},{9,8},{10,9... | collective-permute-start | bytes 393224 | tf_op jit(solution)/shard_map/ppermute | solution.py:30
  102.3 6.2 %collective-permute-start.11 = (f32[128,256]{1,0:T(8,128)S(1)}, f32[128,256]{1,0:T(8,128)S(1)}, u32[]{:S(2)}, u32[]{:S(2)}) collective-permute-start(f32[128,256]{1,0:T(8,128)S(1)} %get-tuple-element.43.refs_1_.refs_5_), channel_id=1, source_target_pairs={{0,1},{1,2},{2,3},{3,4},{4,5},{5,6},{6,7},{7,0},{8,9},{9,10},{10,1... | collective-permute-start | bytes 393224 | tf_op jit(solution)/shard_map/ppermute | solution.py:30
  108.5 5.8 %collective-permute-start.19 = (f32[128,256]{1,0:T(8,128)S(1)}, f32[128,256]{1,0:T(8,128)S(1)}, u32[]{:S(2)}, u32[]{:S(2)}) collective-permute-start(f32[128,256]{1,0:T(8,128)S(1)} %collective-permute-done.12.refs_0_), channel_id=1, source_target_pairs={{0,7},{1,0},{2,1},{3,2},{4,3},{5,4},{6,5},{7,6},{8,15},{9,8},{10,9... | collective-permute-start | bytes 393224 | tf_op jit(solution)/shard_map/ppermute | solution.py:30
  108.6 9.1 %collective-permute-start.18 = (f32[128,256]{1,0:T(8,128)S(1)}, f32[128,256]{1,0:T(8,128)S(1)}, u32[]{:S(2)}, u32[]{:S(2)}) collective-permute-start(f32[128,256]{1,0:T(8,128)S(1)} %collective-permute-done.12.refs_0_), channel_id=1, source_target_pairs={{0,6},{1,7},{2,0},{3,1},{4,2},{5,3},{6,4},{7,5},{8,14},{9,15},{10,... | collective-permute-start | bytes 393224 | tf_op jit(solution)/shard_map/ppermute | solution.py:30
  110.3 8.0 %collective-permute-start.17 = (f32[128,256]{1,0:T(8,128)S(1)}, f32[128,256]{1,0:T(8,128)S(1)}, u32[]{:S(2)}, u32[]{:S(2)}) collective-permute-start(f32[128,256]{1,0:T(8,128)S(1)} %collective-permute-done.13.refs_3_), channel_id=1, source_target_pairs={{0,2},{1,3},{2,4},{3,5},{4,6},{5,7},{6,0},{7,1},{8,10},{9,11},{10,... | collective-permute-start | bytes 393224 | tf_op jit(solution)/shard_map/ppermute | solution.py:30
  111.6 8.6 %collective-permute-start.16 = (f32[128,256]{1,0:T(8,128)S(1)}, f32[128,256]{1,0:T(8,128)S(1)}, u32[]{:S(2)}, u32[]{:S(2)}) collective-permute-start(f32[128,256]{1,0:T(8,128)S(1)} %collective-permute-done.13.refs_3_), channel_id=1, source_target_pairs={{0,1},{1,2},{2,3},{3,4},{4,5},{5,6},{6,7},{7,0},{8,9},{9,10},{10,1... | collective-permute-start | bytes 393224 | tf_op jit(solution)/shard_map/ppermute | solution.py:30
  113.5 23.7 %collective-permute-start.22 = (f32[4,128,256]{2,1,0:T(8,128)S(1)}, f32[4,128,256]{2,1,0:T(8,128)S(1)}, u32[]{:S(2)}, u32[]{:S(2)}) collective-permute-start(f32[4,128,256]{2,1,0:T(8,128)S(1)} %shard_map.84.refs_2_), channel_id=1, source_target_pairs={{0,200},{8,208},{16,216},{24,224},{32,232},{40,240},{48,248},{56,0... | collective-permute-start | bytes 1572872 | tf_op jit(solution)/shard_map/ppermute | solution.py:30
  114.3 22.9 %collective-permute-start.20 = (f32[4,128,256]{2,1,0:T(8,128)S(1)}, f32[4,128,256]{2,1,0:T(8,128)S(1)}, u32[]{:S(2)}, u32[]{:S(2)}) collective-permute-start(f32[4,128,256]{2,1,0:T(8,128)S(1)} %shard_map.84.refs_2_), channel_id=1, source_target_pairs={{0,56},{8,64},{16,72},{24,80},{32,88},{40,96},{48,104},{56,112},{6... | collective-permute-start | bytes 1572872 | tf_op jit(solution)/shard_map/ppermute | solution.py:30
  120.2 17.1 %collective-permute-start.23 = (f32[4,128,256]{2,1,0:T(8,128)S(1)}, f32[4,128,256]{2,1,0:T(8,128)S(1)}, u32[]{:S(2)}, u32[]{:S(2)}) collective-permute-start(f32[4,128,256]{2,1,0:T(8,128)S(1)} %shard_map.85.refs_3_), channel_id=1, source_target_pairs={{0,200},{8,208},{16,216},{24,224},{32,232},{40,240},{48,248},{56,0... | collective-permute-start | bytes 1572872 | tf_op jit(solution)/shard_map/ppermute | solution.py:30
  121.0 16.3 %collective-permute-start.21 = (f32[4,128,256]{2,1,0:T(8,128)S(1)}, f32[4,128,256]{2,1,0:T(8,128)S(1)}, u32[]{:S(2)}, u32[]{:S(2)}) collective-permute-start(f32[4,128,256]{2,1,0:T(8,128)S(1)} %shard_map.85.refs_3_), channel_id=1, source_target_pairs={{0,56},{8,64},{16,72},{24,80},{32,88},{40,96},{48,104},{56,112},{6... | collective-permute-start | bytes 1572872 | tf_op jit(solution)/shard_map/ppermute | solution.py:30
  123.2 13.3 %collective-permute-start.25 = (f32[8,256]{1,0:T(8,128)S(1)}, f32[8,256]{1,0:T(8,128)S(1)}, u32[]{:S(2)}, u32[]{:S(2)}) collective-permute-start(f32[8,256]{1,0:T(8,128)S(1)} %get-tuple-element.52), channel_id=1, source_target_pairs={{8,0},{41,1},{74,2},{107,3},{140,4},{173,5},{206,6},{239,7},{16,8}... | collective-permute-start | bytes 24584 | tf_op jit(solution)/shard_map/ppermute | solution.py:374
  136.6 0.7 collective-permute-start.24
  137.3 12.5 %copy-start.9 = (f32[4,128,256]{2,1,0:T(8,128)}, f32[4,128,256]{2,1,0:T(8,128)S(1)}, u32[]{:S(2)}) copy-start(f32[4,128,256]{2,1,0:T(8,128)S(1)} %collective-permute-done.23.refs_7_) | copy-start | bytes 1572868
  159.4 16.4 %collective-permute-start.26 = (f32[2,136,256]{2,1,0:T(8,128)S(1)}, f32[2,136,256]{2,1,0:T(8,128)S(1)}, u32[]{:S(2)}, u32[]{:S(2)}) collective-permute-start(f32[2,136,256]{2,1,0:T(8,128)S(1)} %get-tuple-element.54), channel_id=1, source_target_pairs={{0,1},{1,2},{2,3},{3,4},{4,5},{5,6},{6,7},{7,0},{8,9},{9,10},{10,1... | collective-permute-start | bytes 835592 | tf_op jit(solution)/shard_map/ppermute | solution.py:30
  160.4 15.3 %collective-permute-start.27 = (f32[2,136,256]{2,1,0:T(8,128)S(1)}, f32[2,136,256]{2,1,0:T(8,128)S(1)}, u32[]{:S(2)}, u32[]{:S(2)}) collective-permute-start(f32[2,136,256]{2,1,0:T(8,128)S(1)} %get-tuple-element.55), channel_id=1, source_target_pairs={{0,7},{1,0},{2,1},{3,2},{4,3},{5,4},{6,5},{7,6},{8,15},{9,8},{10,9... | collective-permute-start | bytes 835592 | tf_op jit(solution)/shard_map/ppermute | solution.py:30
  164.8 10.9 %collective-permute-start.28 = (f32[136,256]{1,0:T(8,128)S(1)}, f32[136,256]{1,0:T(8,128)S(1)}, u32[]{:S(2)}, u32[]{:S(2)}) collective-permute-start(f32[136,256]{1,0:T(8,128)S(1)} %get-tuple-element.58), channel_id=1, source_target_pairs={{0,6},{1,7},{2,0},{3,1},{4,2},{5,3},{6,4},{7,5},{8,14},{9,15},{10,... | collective-permute-start | bytes 417800 | tf_op jit(solution)/shard_map/ppermute | solution.py:30
  175.8 9.1 %collective-permute-start.29 = (f32[136,256]{1,0:T(8,128)S(1)}, f32[136,256]{1,0:T(8,128)S(1)}, u32[]{:S(2)}, u32[]{:S(2)}) collective-permute-start(f32[136,256]{1,0:T(8,128)S(1)} %get-tuple-element.59), channel_id=1, source_target_pairs={{0,2},{1,3},{2,4},{3,5},{4,6},{5,7},{6,0},{7,1},{8,10},{9,11},{10,... | collective-permute-start | bytes 417800 | tf_op jit(solution)/shard_map/ppermute | solution.py:30
  178.6 7.3 %collective-permute-start.30 = (f32[136,256]{1,0:T(8,128)S(1)}, f32[136,256]{1,0:T(8,128)S(1)}, u32[]{:S(2)}, u32[]{:S(2)}) collective-permute-start(f32[136,256]{1,0:T(8,128)S(1)} %get-tuple-element.60), channel_id=1, source_target_pairs={{0,6},{1,7},{2,0},{3,1},{4,2},{5,3},{6,4},{7,5},{8,14},{9,15},{10,... | collective-permute-start | bytes 417800 | tf_op jit(solution)/shard_map/ppermute | solution.py:30
Sparse Core Ops, SparseCore 0:
  22.0 37.7 all-gather.4
  108.6 41.0 all-gather.6
